TPU v7x, 32 devices: a whole 2x2x4 slice. The times are simulated.
32 devices in a mesh: wide: 8 (over z, x), narrow: 4 (over y, core).
Axes of the slice: x: 2, y: 2, z: 4, core: 2. Of those that a mesh axis runs over, the one named last changes fastest.
Arguments:
- token_ids: int32 [128, 64], P(('wide', 'narrow')), may hold values from 0 to 51199
- targets: int32 [128, 64], P(('wide', 'narrow')), may hold values from -1 to 51199, as said below
- joint_weight: float32 [2304, 768], P('narrow'), may hold values from -0.21875 to 0.21875
- output_weight: float32 [768, 768], P('narrow'), may hold values from -0.625 to 0.625
- expand_weight: float32 [3072, 768], P('narrow'), may hold values from -0.21875 to 0.21875
- reduce_weight: float32 [3072, 768], P('narrow'), may hold values from -0.109375 to 0.109375
- joint_velocity: float32 [2304, 768], P('narrow'), may hold values from -4.5776367e-05 to 4.5776367e-05
- output_velocity: float32 [768, 768], P('narrow'), may hold values from -4.5776367e-05 to 4.5776367e-05
- expand_velocity: float32 [3072, 768], P('narrow'), may hold values from -4.5776367e-05 to 4.5776367e-05
- reduce_velocity: float32 [3072, 768], P('narrow'), may hold values from -4.5776367e-05 to 4.5776367e-05
- embedding: float32 [51200, 768], P(('wide', 'narrow')), may hold values from -0.4330127 to 0.4330127
- embed_moment: float32 [51200, 768], P(('wide', 'narrow')), may hold values from -4.7683716e-06 to 4.7683716e-06
- embed_square: float32 [51200, 768], P(('wide', 'narrow')), may hold values from 5.3810434e-14 to 2.1524174e-13
- positions: float32 [64, 768], replicated, may hold values from -1.75 to 1.75
- position_moment: float32 [64, 768], replicated, may hold values from -4.7683716e-06 to 4.7683716e-06
- position_square: float32 [64, 768], replicated, may hold values from 5.3810434e-14 to 2.1524174e-13
- norm_gains: float32 [3, 768], replicated, may hold values from 0.5 to 1.5
- gain_moment: float32 [3, 768], replicated, may hold values from -4.5776367e-05 to 4.5776367e-05
- gain_square: float32 [3, 768], replicated, may hold values from 5.3810433e-12 to 2.1524173e-11
- biases: float32 [8448], replicated, may hold values from -0.625 to 0.625
- bias_moment: float32 [8448], replicated, may hold values from -4.5776367e-05 to 4.5776367e-05
- bias_square: float32 [8448], replicated, may hold values from 5.3810433e-12 to 2.1524173e-11
Outputs:
- loss_sum: float32 [], replicated
- loss_count: float32 [], replicated
- grad_norm: float32 [], replicated
- joint_next: float32 [2304, 768], P('narrow')
- output_next: float32 [768, 768], P('narrow')
- expand_next: float32 [3072, 768], P('narrow')
- reduce_next: float32 [3072, 768], P('narrow')
- joint_carried: float32 [2304, 768], P('narrow')
- output_carried: float32 [768, 768], P('narrow')
- expand_carried: float32 [3072, 768], P('narrow')
- reduce_carried: float32 [3072, 768], P('narrow')
- embed_next: float32 [51200, 768], P(('wide', 'narrow'))
- embed_moments: float32 [51200, 768], P(('wide', 'narrow'))
- embed_squares: float32 [51200, 768], P(('wide', 'narrow'))
- position_next: float32 [64, 768], replicated
- position_moments: float32 [64, 768], replicated
- position_squares: float32 [64, 768], replicated
- gains_next: float32 [3, 768], replicated
- gain_moments: float32 [3, 768], replicated
- gain_squares: float32 [3, 768], replicated
- biases_next: float32 [8448], replicated
- bias_moments: float32 [8448], replicated
- bias_squares: float32 [8448], replicated
Inputs may be any that keep to these rules, and one draw needn't show every extreme that they name: `targets`: -1 marks a position that does not count; at least one position counts.
All inputs are finite; a program needn't handle non-finite values.
Results may differ from a plain program's by a relative error of at most 0.014.
Values may be sent and summed in bfloat16 or wider, within the bound.
A program may use at most 320 MiB of HBM per device.

v0:
```python
import functools
import math

import jax
import jax.numpy as jnp
from jax import lax
from jax.experimental import pallas as pl
from jax.experimental.pallas import tpu as pltpu
from jax.sharding import PartitionSpec as P

HEADS = 12
HEAD = 64
LENGTH = 64
NS_STEPS = 3
STEP = 10


HIGH = lax.Precision.HIGHEST
EPS = 1e-05
CLIP = 0.05
MOMENTUM = 0.95
MUON_RATE = 0.5
DECAY = 0.1
BETA_ONE = 0.9
BETA_TWO = 0.999
EMBED_RATE = 0.02
PLACE_RATE = 0.1
SMALL_RATE = 0.2
NS_A = 3.4445
NS_B = -4.775
NS_C = 2.0315
MESH = pl.DeviceIdType.MESH
MIB = 1 << 20
TOKEN_TILE = 256


def times_t(left, right):
    return lax.dot_general(
        left, right, (((1,), (1,)), ((), ())), preferred_element_type=jnp.float32
    )


def outer_sum(left, right):
    return lax.dot_general(
        left, right, (((0,), (0,)), ((), ())), preferred_element_type=jnp.float32
    )


def plain(left, right):
    return jnp.dot(left, right, preferred_element_type=jnp.float32)


def norm_forward(stream, gain, shift):
    centred = stream - jnp.mean(stream, -1, keepdims=True)
    inverse = lax.rsqrt(jnp.mean(centred * centred, -1, keepdims=True) + EPS)
    normed = centred * inverse
    return (normed * gain + shift, normed, inverse)


def norm_backward(upstream, normed, inverse, gain):
    scaled = upstream * gain
    inner = inverse * (
        scaled
        - jnp.mean(scaled, -1, keepdims=True)
        - normed * jnp.mean(scaled * normed, -1, keepdims=True)
    )
    return (
        inner,
        jnp.sum(upstream * normed, 0, keepdims=True),
        jnp.sum(upstream, 0, keepdims=True),
    )


def gelu_tanh(values):
    return jax.nn.gelu(values, approximate=True)


def column_sum(values):
    return jnp.sum(values.astype(jnp.float32), 0, keepdims=True)


def pair_masks(tokens):
    first = lax.broadcasted_iota(jnp.int32, (tokens, 2 * HEAD), 1) < HEAD
    row = lax.broadcasted_iota(jnp.int32, (tokens, tokens), 0)
    column = lax.broadcasted_iota(jnp.int32, (tokens, tokens), 1)
    return first, (row // LENGTH == column // LENGTH) & (column <= row)


def head_probs(queries, key_heads, seen):
    scores = times_t(queries, key_heads) * HEAD ** (-0.5)
    scores = jnp.where(seen, scores, -1000000000.0)
    powers = jnp.exp(scores - jnp.max(scores, -1, keepdims=True))
    return powers * (1.0 / jnp.sum(powers, -1, keepdims=True))


def forward_kernel(
    x_ref,
    place_ref,
    gain_ref,
    bias_ref,
    joint_hbm,
    output_hbm,
    expand_hbm,
    reduce_hbm,
    low_ref,
    normed_ref,
    inverse_ref,
    joint_out,
    context_ref,
    upward_ref,
    joint_ref,
    output_ref,
    expand_ref,
    reduce_ref,
    load_sem,
):
    pairs = ((joint_hbm, joint_ref), (output_hbm, output_ref), (expand_hbm, expand_ref), (reduce_hbm, reduce_ref))
    loads = [
        pltpu.make_async_copy(source, target, load_sem.at[number])
        for number, (source, target) in enumerate(pairs)
    ]
    for load in loads:
        load.start()
    tokens, width = x_ref.shape

    def norm(number, stream):
        result, normed, inverse = norm_forward(
            stream, gain_ref[number : number + 1, :], bias_ref[number : number + 1, :]
        )
        normed_ref[number] = normed
        inverse_ref[number] = jnp.broadcast_to(inverse, (tokens, 128))
        return result.astype(jnp.bfloat16)

    stream = x_ref[...] + jnp.concatenate([place_ref[...]] * (tokens // LENGTH), 0)
    first_low = norm(0, stream)
    loads[0].wait()
    for part in range(3):
        span = pl.ds(part * width, width)
        result = times_t(first_low, joint_ref[span, :])
        if part != 1:
            row = 3 if part == 0 else 4
            result = result + bias_ref[row : row + 1, :]
        joint_out[:, span] = result.astype(jnp.bfloat16)
    first, seen = pair_masks(tokens)
    zero = jnp.zeros((), jnp.bfloat16)
    for pair in range(HEADS // 2):
        queries = joint_out[:, pl.ds(pair * 128, 128)]
        key_heads = joint_out[:, pl.ds(width + pair * 128, 128)]
        values = joint_out[:, pl.ds(2 * width + pair * 128, 128)]
        parts = []
        for mine in (first, ~first):
            probs = head_probs(jnp.where(mine, queries, zero), key_heads, seen)
            parts.append(plain(probs.astype(jnp.bfloat16), values))
        context_ref[:, pl.ds(pair * 128, 128)] = jnp.where(first, *parts).astype(jnp.bfloat16)
    loads[1].wait()
    stream = stream + times_t(context_ref[...], output_ref[...]) + bias_ref[5:6, :]
    second_low = norm(1, stream)
    stream = stream + bias_ref[6:7, :]
    loads[2].wait()
    loads[3].wait()
    for part in range(expand_ref.shape[0] // width):
        span = pl.ds(part * width, width)
        upward = times_t(second_low, expand_ref[span, :]) + bias_ref[7 + part : 8 + part, :]
        upward_ref[:, span] = upward
        stream = stream + plain(gelu_tanh(upward).astype(jnp.bfloat16), reduce_ref[span, :])
    low_ref[...] = norm(2, stream)


def layer_forward(embedded, positions, norm_gains, bias_rows, weights):
    tokens, width = embedded.shape
    vmem, any_space = pl.BlockSpec(memory_space=pltpu.VMEM), pl.BlockSpec(memory_space=pl.ANY)
    shape = jax.ShapeDtypeStruct
    hidden = weights[2].shape[0]
    return pl.pallas_call(
        forward_kernel,
        out_shape=(
            shape((tokens, width), jnp.bfloat16),
            shape((3, tokens, width), jnp.float32),
            shape((3, tokens, 128), jnp.float32),
            shape((tokens, 3 * width), jnp.bfloat16),
            shape((tokens, width), jnp.bfloat16),
            shape((tokens, hidden), jnp.float32),
        ),
        in_specs=[vmem] * 4 + [any_space] * 4,
        out_specs=[vmem] * 6,
        scratch_shapes=[pltpu.VMEM(w.shape, w.dtype) for w in weights]
        + [pltpu.SemaphoreType.DMA((4,))],
        compiler_params=pltpu.CompilerParams(vmem_limit_bytes=63 * MIB),
        name="layer_forward",
    )(embedded, positions, norm_gains, bias_rows, *weights)


def gelu_slope(values):
    inner = math.sqrt(2.0 / math.pi)
    squared = values * values
    bent = jnp.tanh(inner * (values + 0.044715 * squared * values))
    return 0.5 * values * (1.0 + bent), 0.5 * (1.0 + bent) + 0.5 * values * (
        1.0 - bent * bent
    ) * (inner * (1.0 + 3 * 0.044715 * squared))


def backward_flow(ins, outs, scratch):
    (final_ref, gain_ref, bias_ref, normed_ref, inverse_ref, joint_in, context_ref, upward_ref) = ins
    (stream_ref, small_ref, front_ref, expand_out, reduce_out) = outs
    (joint_ref, output_ref, expand_ref, reduce_ref, waits) = scratch
    hold = reduce_ref
    tokens, width = final_ref.shape
    _, ups, height, _ = front_ref.shape
    groups = 2 * ups

    def put(ref, start, grad):
        for group in range(groups):
            low = max(group * height, start)
            high = min((group + 1) * height, start + grad.shape[0])
            if low < high:
                ref[group % 2, group // 2, pl.ds(low - group * height, high - low), :] = grad[
                    low - start : high - start
                ]

    def gain(number):
        return gain_ref[number : number + 1, :]

    def normed_low(number):
        return (normed_ref[number] * gain(number) + bias_ref[number : number + 1, :]).astype(
            jnp.bfloat16
        )

    def back(number, upstream):
        inner, gain_row, shift_row = norm_backward(
            upstream, normed_ref[number], inverse_ref[number][:, :1], gain(number)
        )
        small_ref[number : number + 1, :] = gain_row
        small_ref[3 + number : 4 + number, :] = shift_row
        return inner

    small_ref[...] = jnp.zeros_like(small_ref)
    back_f = back(2, final_ref[...])
    down = back_f.astype(jnp.bfloat16)
    small_ref[9:10, :] = column_sum(down)
    second_low = normed_low(1)
    second_grad = jnp.zeros((tokens, width), jnp.float32)
    waits[2].wait()
    waits[3].wait()
    for part in range(expand_ref.shape[0] // width):
        span = pl.ds(part * width, width)
        active, slope = gelu_slope(upward_ref[:, span])
        upward_grad = (times_t(down, reduce_ref[span, :]) * slope).astype(jnp.bfloat16)
        small_ref[10 + part : 11 + part, :] = column_sum(upward_grad)
        second_grad = second_grad + plain(upward_grad, expand_ref[span, :])
        put(expand_out, part * width, outer_sum(upward_grad, second_low).astype(jnp.bfloat16))
        put(reduce_out, part * width, outer_sum(active.astype(jnp.bfloat16), down).astype(jnp.bfloat16))
    yield 0.0
    mid_grad = back_f + back(1, second_grad)
    stream_ref[...] = mid_grad
    attn_grad = mid_grad.astype(jnp.bfloat16)
    small_ref[8:9, :] = column_sum(attn_grad)
    waits[1].wait()
    last = pl.ds(3 * tokens, tokens)
    hold[last, :] = plain(attn_grad, output_ref[...]).astype(jnp.bfloat16)
    output_grad = outer_sum(attn_grad, context_ref[...]).astype(jnp.bfloat16)
    rows = width // groups
    joint_rows = height - rows
    for group in range(groups):
        front_ref[group % 2, group // 2, pl.ds(joint_rows, rows), :] = output_grad[
            group * rows : (group + 1) * rows
        ]
    yield 2.0
    first, seen = pair_masks(tokens)
    zero = jnp.zeros((), jnp.bfloat16)
    for pair in range(HEADS // 2):
        spans = [pl.ds(part * width + pair * 128, 128) for part in range(3)]
        queries, key_heads, values = (joint_in[:, span] for span in spans)
        upstream = hold[last, spans[0]]
        parts = []
        for mine in (first, ~first):
            probs = head_probs(jnp.where(mine, queries, zero), key_heads, seen)
            probs_grad = times_t(jnp.where(mine, upstream, zero), values)
            score_grad = (
                probs * (probs_grad - jnp.sum(probs * probs_grad, -1, keepdims=True))
            ).astype(jnp.bfloat16)
            parts.append(
                (
                    plain(score_grad, key_heads) * HEAD ** (-0.5),
                    outer_sum(score_grad, queries) * HEAD ** (-0.5),
                    outer_sum(probs.astype(jnp.bfloat16), upstream),
                )
            )
        for part, (one, two) in enumerate(zip(*parts)):
            hold[pl.ds(part * tokens, tokens), spans[0]] = jnp.where(first, one, two).astype(
                jnp.bfloat16
            )
        yield 1.5
    first_low = normed_low(0)
    waits[0].wait()
    first_grad = jnp.zeros((tokens, width), jnp.float32)
    for part in range(3):
        span = pl.ds(part * width, width)
        piece = hold[pl.ds(part * tokens, tokens), :]
        if part != 1:
            row = 6 if part == 0 else 7
            small_ref[row : row + 1, :] = column_sum(piece)
        first_grad = first_grad + plain(piece, joint_ref[span, :])
        grad = outer_sum(piece, first_low).astype(jnp.bfloat16)
        for group in range(groups):
            start = max(group * joint_rows, part * width)
            end = min((group + 1) * joint_rows, (part + 1) * width)
            if start < end:
                front_ref[
                    group % 2, group // 2, pl.ds(start - group * joint_rows, end - start), :
                ] = grad[start - part * width : end - part * width]
        yield 1.5
    stream = stream_ref[...] + back(0, first_grad)
    stream_ref[...] = stream
    placed = stream[:LENGTH]
    for sequence in range(1, tokens // LENGTH):
        placed = placed + stream[sequence * LENGTH : (sequence + 1) * LENGTH]
    small_ref[14 : 14 + LENGTH, :] = placed


def adam_step(weight, moment, square, gradient, rate, decay):
    moment = BETA_ONE * moment + (1 - BETA_ONE) * gradient
    square = BETA_TWO * square + (1 - BETA_TWO) * gradient * gradient
    unbiased = moment / (1 - BETA_ONE**STEP)
    spread = square / (1 - BETA_TWO**STEP)
    return (
        weight - rate * (unbiased / (jnp.sqrt(spread) + 1e-08) + decay * weight),
        moment,
        square,
    )


def log_two(size):
    return size.bit_length() - 1


def lanes():
    wide, narrow = lax.axis_size("wide"), lax.axis_size("narrow")
    across = wide // 4
    x_bits = [("wide", 1 << i) for i in range(log_two(across))]
    z_bits = [("wide", across << i) for i in range(log_two(wide // across))]
    y_bits = [("narrow", 2 << i) for i in range(log_two(narrow // 2))]
    return ("narrow", 1), x_bits, y_bits, z_bits


def swap(array, bit):
    axis, mask = bit
    return lax.ppermute(array, axis, [(i, i ^ mask) for i in range(lax.axis_size(axis))])


def side(bit):
    axis, mask = bit
    return (lax.axis_index(axis) // mask) % 2


def join(mine, other, bit, dim=0):
    own = side(bit)
    return jnp.where(
        own == 0, jnp.concatenate([mine, other], dim), jnp.concatenate([other, mine], dim)
    )


def halves(array, bit):
    own = side(bit)
    half = array.shape[0] // 2
    keep = lax.dynamic_slice_in_dim(array, own * half, half)
    send = lax.dynamic_slice_in_dim(array, (1 - own) * half, half)
    return keep, send


def group_bits():
    _, _, y_bits, z_bits = lanes()
    return z_bits + y_bits


SPREAD_ORDERS = ("nyf", "fny", "nfy", "fyn")
COLLECT_ORDERS = ("yfn", "ynf", "nyf", "fyn")


def routes(rows, orders):
    _, _, y_bits, z_bits = lanes()
    kinds = {"y": y_bits, "n": z_bits[:1], "f": z_bits[1:]}
    size = rows // len(orders)
    return [
        (number * size, size, [bit for kind in order for bit in kinds[kind]])
        for number, order in enumerate(orders)
    ]


def flat_mask(bit):
    axis, mask = bit
    return mask * lax.axis_size("narrow") if axis == "wide" else mask


def group_masks():
    masks = [0]
    for bit in group_bits():
        masks = masks + [other ^ flat_mask(bit) for other in masks]
    return masks


def neighbour(bit):
    axis, mask = bit
    wide, narrow = lax.axis_index("wide"), lax.axis_index("narrow")
    if axis == "wide":
        return wide + mask * (1 - 2 * ((wide // mask) % 2)), narrow
    return wide, narrow + mask * (1 - 2 * ((narrow // mask) % 2))


def greet(devices):
    barrier = pltpu.get_barrier_semaphore()
    for device in devices:
        pl.semaphore_signal(barrier, inc=1, device_id=device, device_id_type=MESH)
    pl.semaphore_wait(barrier, len(devices))


class Mail:
    def __init__(self, send_sem, recv_sem, lane_bits):
        core, x_bits, y_bits, z_bits = lane_bits
        self.send_sem, self.recv_sem = send_sem, recv_sem
        self.used, self.sent, self.open = 0, [], []
        self.links = {core: (("core", 1 / 600e3),)}
        self.links.update({bit: (("x", 2 / 91e3),) for bit in x_bits})
        self.links.update({bit: (("y", 2 / 91e3),) for bit in y_bits})
        self.links.update({bit: (("z", 2 / 91e3),) for bit in z_bits[:1]})
        self.links.update({bit: (("z", 2 / 91e3), ("far", 4 / 91e3)) for bit in z_bits[1:]})
        self.free, self.now, self.ready = {}, 0.0, []

    def expect(self, source, bit):
        size = math.prod(source.shape) * source.dtype.itemsize
        due = self.now
        for link, rate in self.links[bit]:
            self.free[link] = max(self.free.get(link, 0.0), self.now) + size * rate
            due = max(due, self.free[link])
        return due + 3.5

    def post(self, source, target, bit):
        copy = pltpu.make_async_remote_copy(
            src_ref=source,
            dst_ref=target,
            send_sem=self.send_sem.at[self.used],
            recv_sem=self.recv_sem.at[self.used],
            device_id=neighbour(bit),
            device_id_type=MESH,
        )
        copy.start()
        self.due = self.expect(source, bit)
        self.used += 1
        self.sent.append(copy)
        self.open.append(copy)
        return copy

    def keep(self, source, target):
        copy = pltpu.make_async_copy(source, target, self.recv_sem.at[self.used])
        copy.start()
        self.used += 1
        self.open.append(copy)
        return copy

    def take(self, copy):
        if any(other is copy for other in self.open):
            self.open = [other for other in self.open if other is not copy]
            if any(other is copy for other in self.sent):
                copy.wait_recv()
            else:
                copy.wait()

    def spend(self, time):
        self.now += time
        return self.now

    def run(self, flows):
        waiting = [(next(flow, None), flow) for flow in flows]
        while True:
            waiting += [(next(flow, None), flow) for flow in self.ready]
            self.ready = []
            waiting = [entry for entry in waiting if entry[0] is not None]
            if not waiting:
                return
            place = min(range(len(waiting)), key=lambda i: waiting[i][0])
            due, flow = waiting.pop(place)
            self.now = max(self.now, due) + 0.4
            waiting.append((next(flow, None), flow))

    def close(self):
        for copy in list(self.open):
            self.take(copy)
        for copy in self.sent:
            copy.wait_send()


def mail_sems(count):
    return [pltpu.SemaphoreType.DMA((count,)), pltpu.SemaphoreType.DMA((count,))]


def spread_flow(mail, bits, part, x_ref, out_ref):
    first, rows, order = part
    span = pl.ds(first, rows)
    held = {0: None}
    for bit in order:
        step = 1 << bits.index(bit)
        for block in list(held):
            if block:
                mail.take(held[block])
            source = out_ref.at[block, span] if block else x_ref.at[span]
            held[block ^ step] = mail.post(source, out_ref.at[block ^ step, span], bit)
        yield mail.due


def spread_kernel(lane_bits, plan, x_ref, out_ref, send_sem, recv_sem):
    bits = lane_bits[3] + lane_bits[2]
    greet([neighbour(bit) for bit in bits])
    mail = Mail(send_sem, recv_sem, lane_bits)
    mail.run([spread_flow(mail, bits, part, x_ref, out_ref) for part in plan])
    mail.keep(x_ref, out_ref.at[0])
    mail.close()


def spread(array):
    bits, plan = group_bits(), routes(array.shape[0], SPREAD_ORDERS)
    count = 1 << len(bits)
    return pl.pallas_call(
        functools.partial(spread_kernel, lanes(), plan),
        out_shape=jax.ShapeDtypeStruct((count,) + array.shape, array.dtype),
        in_specs=[pl.BlockSpec(memory_space=pltpu.VMEM)],
        out_specs=pl.BlockSpec(memory_space=pl.ANY),
        scratch_shapes=mail_sems(len(plan) * count),
        compiler_params=pltpu.CompilerParams(
            collective_id=4, has_side_effects=True, vmem_limit_bytes=62 * MIB
        ),
        name="rows_spread",
    )(array)


def collect_flow(mail, bits, part, refs):
    first, rows, order = part
    x_ref, out_ref, sum_ref, got_ref = refs
    span = pl.ds(first, rows)
    held = list(range(1 << len(bits)))
    for stage, bit in enumerate(order):
        step = 1 << bits.index(bit)
        source = sum_ref if stage else x_ref
        held = [block for block in held if not block & step]
        base = (1 << len(bits)) - 2 * len(held)
        copies = [
            mail.post(source.at[block ^ step, span], got_ref.at[base + place, span], bit)
            for place, block in enumerate(held)
        ]
        yield mail.due
        for place, (block, copy) in enumerate(zip(held, copies)):
            mail.take(copy)
            total = source[block, span, :].astype(jnp.float32) + got_ref[
                base + place, span, :
            ].astype(jnp.float32)
            if stage == len(bits) - 1:
                out_ref[span, :] = total
            else:
                sum_ref[block, span, :] = total.astype(jnp.bfloat16)


def head_back_kernel(lane_bits, plan, tile, x_ref, *refs):
    core, _, y_bits, z_bits = lane_bits
    bits = z_bits + y_bits
    if tile:
        slope_ref, rows_ref, out_ref, keep_ref, pass_ref = refs[:5]
        sum_ref, got_ref, send_sem, recv_sem = refs[5:9]
        loads, sent_ref, other_ref, load_sem = refs[9:]
        half = sent_ref.shape[0]
        count = half // tile
        order = [count + i for i in range(count)] + [count - 1 - i for i in range(count)]

        def load(number):
            return pltpu.make_async_copy(
                slope_ref.at[:, pl.ds(order[number] * tile, tile)],
                loads.at[number % 2],
                load_sem.at[number % 2],
            )

        load(0).start()
        greet([neighbour(bit) for bit in bits + [core]])
    else:
        out_ref, sum_ref, got_ref, send_sem, recv_sem = refs
        greet([neighbour(bit) for bit in bits])
    mail = Mail(send_sem, recv_sem, lane_bits)
    flows = [
        collect_flow(mail, bits, part, (x_ref, out_ref, sum_ref, got_ref)) for part in plan
    ]
    if tile:

        def table_flow():
            arrivals = {}
            border = keep_ref.shape[0]
            for number, block in enumerate(order):
                if number + 1 < len(order):
                    load(number + 1).start()
                load(number).wait()
                grad = lax.dot_general(
                    loads[number % 2],
                    rows_ref[...],
                    (((0,), (0,)), ((), ())),
                    preferred_element_type=jnp.float32,
                )
                start = block * tile % half
                span = pl.ds(start, tile)
                if block >= count:
                    sent_ref[span, :] = grad.astype(jnp.bfloat16)
                    arrivals[start] = mail.post(sent_ref.at[span], other_ref.at[span], core)
                else:
                    mail.take(arrivals[start])
                    grad = grad + other_ref[span, :].astype(jnp.float32)
                    lower = min(max(border - start, 0), tile)
                    if lower:
                        keep_ref[pl.ds(start, lower), :] = grad[:lower]
                    if lower < tile:
                        pass_ref[pl.ds(start + lower - border, tile - lower), :] = grad[
                            lower:
                        ].astype(jnp.bfloat16)
                yield mail.spend(2.7)

        flows.append(table_flow())
    mail.run(flows)
    mail.close()


def head_back(array, slopes, group_rows):
    lane_bits = lanes()
    bits, plan = group_bits(), routes(array.shape[1], COLLECT_ORDERS)
    count, rows, width = array.shape
    vocab = slopes.shape[1]
    half = vocab // 2
    tile = 640 if half % 640 == 0 else 0
    vmem = pl.BlockSpec(memory_space=pltpu.VMEM)
    shapes = [jax.ShapeDtypeStruct((rows, width), jnp.float32)]
    scratch = [
        pltpu.VMEM((count, rows, width), jnp.bfloat16),
        pltpu.VMEM((count - 1, rows, width), jnp.bfloat16),
    ] + mail_sems(len(plan) * count + (half // tile if tile else 0))
    operands, specs = [array], [vmem]
    if tile:
        shapes += [
            jax.ShapeDtypeStruct((half // 2, width), jnp.float32),
            jax.ShapeDtypeStruct((half // 2, width), jnp.bfloat16),
        ]
        scratch += [
            pltpu.VMEM((2, slopes.shape[0], tile), jnp.bfloat16),
            pltpu.VMEM((half, width), jnp.bfloat16),
            pltpu.VMEM((half, width), jnp.bfloat16),
            pltpu.SemaphoreType.DMA((2,)),
        ]
        operands += [slopes, group_rows]
        specs += [pl.BlockSpec(memory_space=pl.ANY), vmem]
    outs = pl.pallas_call(
        functools.partial(head_back_kernel, lane_bits, plan, tile),
        out_shape=shapes,
        in_specs=specs,
        out_specs=[vmem] * len(shapes),
        scratch_shapes=scratch,
        compiler_params=pltpu.CompilerParams(
            collective_id=5, has_side_effects=True, vmem_limit_bytes=56 * MIB
        ),
        name="head_back",
    )(*operands)
    if tile:
        return outs
    core = lane_bits[0]
    other = swap(outer_sum(slopes[:, half:], group_rows).astype(jnp.bfloat16), core)
    table_sum = outer_sum(slopes[:, :half], group_rows) + other.astype(jnp.float32)
    return outs[0], table_sum[: half // 2], table_sum[half // 2 :].astype(jnp.bfloat16)


def chip_sizes():
    wides, groups = lax.axis_size("wide"), lax.axis_size("narrow")
    return wides, groups // 2


class Rows:
    def __init__(self, sizes, x_ref, out_ref, send_sem, recv_sem):
        self.sizes, self.x_ref, self.out_ref = sizes, x_ref, out_ref
        self.send_sem, self.recv_sem = send_sem, recv_sem
        self.count = sizes[0] * sizes[1]
        self.place = Place(sizes[0], 2 * sizes[1])

    def peer(self, k):
        ups = self.sizes[1]
        return self.place.peer(k // ups, 2 * (k % ups))

    def each(self, step):
        for k in range(1, self.count):
            step(k)

    def copy(self, k):
        return pltpu.make_async_remote_copy(
            src_ref=self.x_ref.at[k],
            dst_ref=self.out_ref.at[k],
            send_sem=self.send_sem.at[k],
            recv_sem=self.recv_sem.at[k],
            device_id=self.peer(k),
            device_id_type=MESH,
        )

    def greet(self, others):
        self.call(others)
        self.meet(others)

    def call(self, others):
        barrier = pltpu.get_barrier_semaphore()
        self.each(
            lambda k: pl.semaphore_signal(
                barrier, inc=1, device_id=self.peer(k), device_id_type=MESH
            )
        )
        for device in others:
            pl.semaphore_signal(barrier, inc=1, device_id=device, device_id_type=MESH)

    def meet(self, others):
        pl.semaphore_wait(pltpu.get_barrier_semaphore(), self.count - 1 + len(others))

    def start(self):
        self.each(lambda k: self.copy(k).start())

    def own(self):
        return pltpu.make_async_copy(self.x_ref.at[0], self.out_ref.at[0], self.recv_sem.at[0])


def swap_rows_kernel(sizes, x_ref, out_ref, send_sem, recv_sem):
    rows = Rows(sizes, x_ref, out_ref, send_sem, recv_sem)
    rows.greet([])
    rows.start()
    own = rows.own()
    own.start()
    own.wait()
    rows.each(lambda k: rows.copy(k).wait())


def swap_rows(rows):
    sizes = chip_sizes()
    count = sizes[0] * sizes[1]
    return pl.pallas_call(
        functools.partial(swap_rows_kernel, sizes),
        out_shape=jax.ShapeDtypeStruct(rows.shape, rows.dtype),
        in_specs=[pl.BlockSpec(memory_space=pltpu.VMEM)],
        out_specs=pl.BlockSpec(memory_space=pl.ANY),
        scratch_shapes=mail_sems(count),
        compiler_params=pltpu.CompilerParams(collective_id=2, has_side_effects=True),
        name="token_rows",
    )(rows)


def load_kernel(sizes, lane_bits, *refs):
    core, x_bits, y_bits, z_bits = lane_bits
    near = z_bits[0]
    table_ref, weight_refs, rows_ref = refs[0], refs[1:5], refs[5]
    table_out, weight_outs, rows_out = refs[6], refs[7:11], refs[11]
    send_sem, recv_sem, rows_send, rows_recv, pass_send, pass_recv = refs[12:]
    wide, narrow = lax.axis_index("wide"), lax.axis_index("narrow")
    rows = Rows(sizes, rows_ref, rows_out.at[0], rows_send, rows_recv)
    rows.greet([neighbour(core)])
    mail = Mail(send_sem, recv_sem, lane_bits)
    side_near = (wide // near[1]) % 2

    def part(ref, number, half):
        count = ref.shape[1] // 2
        return ref.at[number, pl.ds(pl.multiple_of(half * count, 16), count)]

    def own_part(ref, half):
        count = ref.shape[0] // 2
        return ref.at[pl.ds(pl.multiple_of(half * count, 16), count)]

    tables = {0: mail.keep(table_ref, table_out.at[0, 0])}
    if x_bits:
        tables[1] = mail.post(table_ref, table_out.at[0, 1], x_bits[0])
    held = [0]
    first = []
    for ref, out in zip(weight_refs, weight_outs):
        if y_bits:
            first.append(
                mail.post(own_part(ref, side_near), part(out, narrow, side_near), y_bits[0])
            )
    rows.start()
    own_rows = rows.own()
    own_rows.start()
    mail.post(table_ref, table_out.at[1, 0], core)
    for ref, out in zip(weight_refs, weight_outs):
        mail.keep(ref, out.at[narrow])
        mail.post(ref, out.at[narrow], core)
    own_rows.wait()
    place = narrow
    blocks = [narrow]
    for level, bit in enumerate(y_bits):
        fresh = []
        arrivals = []
        for number, (ref, out) in enumerate(zip(weight_refs, weight_outs)):
            for spot, block in enumerate(blocks):
                other = block + bit[1] * (1 - 2 * ((block // bit[1]) % 2))
                if level == 0:
                    copy = first[number]
                else:
                    copy = mail.post(
                        part(out, block, side_near), part(out, block, side_near), bit
                    )
                arrivals.append((out, other, copy))
                if number == 0:
                    fresh.append(other)
        seconds = []
        for out, other, copy in arrivals:
            mail.take(copy)
            seconds.append(
                mail.post(part(out, other, side_near), part(out, other, side_near), near)
            )
            mail.post(part(out, other, side_near), part(out, other, side_near), core)
        for (out, other, _), copy in zip(arrivals, seconds):
            mail.take(copy)
            mail.post(part(out, other, 1 - side_near), part(out, other, 1 - side_near), core)
        blocks = blocks + fresh

    def hand(k):
        return pltpu.make_async_remote_copy(
            src_ref=rows_out.at[0, k],
            dst_ref=rows_out.at[1, k],
            send_sem=pass_send.at[k],
            recv_sem=pass_recv.at[k],
            device_id=neighbour(core),
            device_id_type=MESH,
        )

    hand(0).start()

    def forward(k):
        rows.copy(k).wait()
        hand(k).start()

    rows.each(forward)
    for level, bit in enumerate(x_bits):
        for block in range(1 << level):
            spot = block + (1 << level)
            if spot not in tables:
                tables[spot] = mail.post(table_out.at[0, block], table_out.at[0, spot], bit)
        for block in range(1 << level):
            spot = block + (1 << level)
            mail.take(tables[spot])
            mail.post(table_out.at[0, spot], table_out.at[1, spot], core)
    hand(0).wait()
    rows.each(lambda k: hand(k).wait())
    mail.close()


def load_all(table, weights, rows):
    lane_bits = lanes()
    sizes = chip_sizes()
    count = sizes[0] * sizes[1]
    groups = lax.axis_size("narrow")
    across = 1 << len(lane_bits[1])
    any_space = pl.BlockSpec(memory_space=pl.ANY)
    shapes = (
        [jax.ShapeDtypeStruct((2, across) + table.shape, table.dtype)]
        + [jax.ShapeDtypeStruct((groups,) + w.shape, w.dtype) for w in weights]
        + [jax.ShapeDtypeStruct((2,) + rows.shape, rows.dtype)]
    )
    table_all, *weights_all, rows_all = pl.pallas_call(
        functools.partial(load_kernel, sizes, lane_bits),
        out_shape=shapes,
        in_specs=[pl.BlockSpec(memory_space=pltpu.VMEM)] * 6,
        out_specs=[any_space] * 6,
        scratch_shapes=mail_sems(8 * 2 * groups + 2 * across + 4)
        + mail_sems(count)
        + mail_sems(count),
        compiler_params=pltpu.CompilerParams(
            collective_id=6, has_side_effects=True, vmem_limit_bytes=62 * MIB
        ),
        name="load_rows",
    )(table, *weights, rows)
    model = table.shape[1]
    return (
        table_all.reshape(-1, model),
        tuple(w.reshape(-1, model) for w in weights_all),
        rows_all,
    )


def tile_of(rows):
    return next(size for size in (128, 96, 64, 48, 32, 16) if rows % size == 0)


def back_reduce_kernel(sizes, lane_bits, kinds, *refs):
    core, x_bits, y_bits, z_bits = lane_bits
    ins, wanted_ref, hbm = refs[:8], refs[8], refs[9:13]
    out_refs, small_out, rows_out, square_out, low_out = refs[13:16], *refs[16:20]
    scratch = refs[20:]
    weights, load_sem, stream_ref, small_ref = scratch[:4], scratch[4], scratch[5], small_out
    grad_refs = scratch[6:9]
    both_ref, core_got = scratch[9:11]
    small_sum, small_got, send_sem, recv_sem, rows_send, rows_recv = scratch[11:17]
    rest = scratch[17:]
    got_refs = []
    for _, _, _, path in kinds:
        got_refs.append(rest[: len(path) + 1])
        rest = rest[len(path) + 1 :]
    waits = [
        pltpu.make_async_copy(source, target, load_sem.at[number])
        for number, (source, target) in enumerate(zip(hbm, weights))
    ]
    for load in waits:
        load.start()
    place = {"wide": lax.axis_index("wide"), "narrow": lax.axis_index("narrow")}
    rows = Rows(sizes, both_ref.at[0], rows_out, rows_send, rows_recv)
    rows.call([neighbour(core)])
    mail = Mail(send_sem, recv_sem, lane_bits)
    ups = grad_refs[0].shape[1]
    own = place["narrow"] % 2
    square_out[...] = jnp.zeros_like(square_out)

    def side_of(bit):
        return (place[bit[0]] // bit[1]) % 2

    def add(total_ref, got_ref, box):
        up, ups_here, first, height = box
        tile = tile_of(height)

        def step(i, carry):
            at = i // (height // tile)
            down = (i % (height // tile)) * tile
            span = pl.ds(pl.multiple_of(first + down, 16), tile)
            got = got_ref[at, pl.ds(pl.multiple_of(down, 16), tile), :]
            total = total_ref[own, up + at, span, :].astype(jnp.float32) + got.astype(jnp.float32)
            total_ref[own, up + at, span, :] = total.astype(jnp.bfloat16)
            return carry

        lax.fori_loop(0, ups_here * (height // tile), step, 0)

    def view(ref, box):
        up, ups_here, first, height = box
        return ref.at[own, pl.ds(up, ups_here), pl.ds(pl.multiple_of(first, 16), height)]

    def flow(number):
        which, offset, height, path = kinds[number]
        total_ref, got, out_ref = grad_refs[which], got_refs[number], out_refs[which]
        span = pl.ds(offset, height)
        copy = mail.post(total_ref.at[1 - own, :, span], got[0], core)
        yield mail.due
        mail.take(copy)
        box = (0, ups, offset, height)
        add(total_ref, got[0], box)
        for stage, (bit, halve) in enumerate(path):
            up, ups_here, first, height = box
            side = side_of(bit)
            if bit[0] == "narrow":
                half = ups_here // 2
                mine = (up + side * half, half, first, height)
                theirs = (up + (1 - side) * half, half, first, height)
            elif halve:
                half = height // 2
                mine = (up, ups_here, first + side * half, half)
                theirs = (up, ups_here, first + (1 - side) * half, half)
            else:
                mine = theirs = box
            copy = mail.post(view(total_ref, theirs), got[stage + 1], bit)
            yield mail.due
            mail.take(copy)
            if not halve:
                copy.wait_send()
                mail.sent = [other for other in mail.sent if other is not copy]
            box = mine
            add(total_ref, got[stage + 1], box)
        up, _, first, height = box
        piece = total_ref[own, up, pl.ds(pl.multiple_of(first, 16), height), :]
        out_ref[pl.ds(pl.multiple_of(first, 16), height), :] = piece
        full = piece.astype(jnp.float32)
        square_out[...] += jnp.sum((full * full).reshape(height // 8, 8, -1), 0)
        for bit, halve in reversed(path):
            if bit[0] == "wide" and halve:
                span = pl.ds(pl.multiple_of(first, 16), height)
                copy = mail.post(out_ref.at[span], out_ref.at[span], bit)
                yield mail.due
                mail.take(copy)
                first = first - side_of(bit) * height
                height = 2 * height

    def small_flow():
        bits = [core] + x_bits + y_bits + z_bits
        small_sum[0] = small_ref[...].astype(jnp.bfloat16)
        for stage, bit in enumerate(bits):
            copy = mail.post(small_sum.at[stage], small_got.at[stage], bit)
            yield mail.due
            mail.take(copy)
            total = small_sum[stage].astype(jnp.float32) + small_got[stage].astype(jnp.float32)
            if stage == len(bits) - 1:
                small_out[...] = total
            else:
                small_sum[stage + 1] = total.astype(jnp.bfloat16)

    def rows_flow():
        low = stream_ref[...].astype(jnp.bfloat16)
        low_out[...] = low
        both = outer_sum(wanted_ref[...], low).astype(jnp.bfloat16)
        both_ref[...] = both.reshape(both_ref.shape)
        copy = mail.post(both_ref.at[1], core_got, core)
        yield mail.due
        mail.take(copy)
        summed = both_ref[0].astype(jnp.float32) + core_got[...].astype(jnp.float32)
        both_ref[0] = summed.astype(jnp.bfloat16)
        rows.start()
        own_rows = rows.own()
        own_rows.start()
        yield mail.due
        own_rows.wait()

    back = backward_flow(
        ins,
        (stream_ref, small_ref) + tuple(grad_refs),
        (*weights, waits),
    )
    next(back)
    rows.meet([neighbour(core)])

    def back_flow():
        for cost in back:
            yield mail.spend(cost)
        mail.ready += [flow(number) for number in range(4, len(kinds))]
        mail.ready += [rows_flow(), small_flow()]

    mail.run([flow(number) for number in range(4)] + [back_flow()])
    rows.each(lambda k: rows.copy(k).wait())
    mail.close()


def back_reduce(final_grad, norm_gains, bias_rows, saved, weights, wanted):
    lane_bits = lanes()
    core, x_bits, y_bits, z_bits = lane_bits
    sizes = chip_sizes()
    tokens, width = final_grad.shape
    ups = sizes[1]
    height = 4 * width // (2 * ups)
    half = height // 2
    bits = {"x": x_bits, "y": y_bits[::-1], "z": z_bits[:1], "f": z_bits[1:]}
    kinds, got_shapes = [], []
    for which, offset, order in (
        (1, 0, "yzfx"),
        (2, 0, "yxzf"),
        (1, half, "yzxf"),
        (2, half, "zyxf"),
        (0, 0, "yxfz"),
        (0, half, "yxzf"),
    ):
        path, ups_here, height_here = [], ups, half
        shapes = [(ups_here, height_here, width)]
        for bit in [bit for kind in order for bit in bits[kind]]:
            halve = True
            if bit[0] == "narrow":
                ups_here //= 2
            else:
                halve = (height_here // 2) % 16 == 0
                height_here = height_here // 2 if halve else height_here
            path.append((bit, halve))
            shapes.append((ups_here, height_here, width))
        kinds.append((which, offset, half, path))
        got_shapes += shapes
    count = sizes[0] * sizes[1]
    steps = 1 + len(kinds[0][3])
    small_rows = 14 + LENGTH
    small = (small_rows + -small_rows % 16, width)
    row_shape = (count, slots(), width)
    vmem, any_space = pl.BlockSpec(memory_space=pltpu.VMEM), pl.BlockSpec(memory_space=pl.ANY)
    shape, low = jax.ShapeDtypeStruct, jnp.bfloat16
    outs = pl.pallas_call(
        functools.partial(back_reduce_kernel, sizes, lane_bits, kinds),
        out_shape=[shape((height, width), low)] * 3
        + [
            shape(small, jnp.float32),
            shape(row_shape, low),
            shape((8, width), jnp.float32),
            shape((tokens, width), low),
        ],
        in_specs=[vmem] * 9 + [any_space] * 4,
        out_specs=[vmem] * 4 + [any_space, vmem, vmem],
        scratch_shapes=[pltpu.VMEM(w.shape, w.dtype) for w in weights]
        + [
            pltpu.SemaphoreType.DMA((4,)),
            pltpu.VMEM((tokens, width), jnp.float32),
        ]
        + [pltpu.VMEM((2, ups, height, width), low) for _ in range(3)]
        + [pltpu.VMEM((2,) + row_shape, low), pltpu.VMEM(row_shape, low)]
        + [pltpu.VMEM((steps,) + small, low), pltpu.VMEM((steps,) + small, low)]
        + mail_sems(len(kinds) * 2 * steps + steps + 1)
        + mail_sems(count)
        + [pltpu.VMEM(one, low) for one in got_shapes],
        compiler_params=pltpu.CompilerParams(
            collective_id=7, has_side_effects=True, vmem_limit_bytes=63 * MIB
        ),
        name="back_reduce",
    )(final_grad, norm_gains, bias_rows, *saved, wanted, *weights)
    repeats = 1
    for bit, halve in kinds[0][3]:
        repeats *= 1 if halve else 2
    return outs[:3], outs[3], outs[4], outs[5] / repeats, outs[6]


class Place:
    def __init__(self, wides, groups):
        self.wide, self.narrow = lax.axis_index("wide"), lax.axis_index("narrow")
        self.wide_steps = self.steps(self.wide, wides)
        self.narrow_steps = self.steps(self.narrow, groups)

    def steps(self, place, size):
        masks = [1 << bit for bit in range(log_two(size))]
        return {mask: mask * (1 - 2 * ((place // mask) % 2)) for mask in masks}

    def peer(self, wide_mask, narrow_mask):
        wide, narrow = self.wide, self.narrow
        for mask, step in self.wide_steps.items():
            wide = wide + step if mask & wide_mask else wide
        for mask, step in self.narrow_steps.items():
            narrow = narrow + step if mask & narrow_mask else narrow
        return wide, narrow


def exchange_kernel(masks, sizes, whole, x_ref, out_ref, send_sem, recv_sem, own_sem):
    wides, groups = sizes
    place = Place(wides, groups)
    masks = list(range(wides * groups)) if masks is None else masks
    count = len(masks)

    def peer(mask):
        return place.peer(mask // groups, mask % groups)

    def each(step):
        for k in range(1, count):
            step(k, masks[k])

    def copy(k, mask):
        return pltpu.make_async_remote_copy(
            src_ref=x_ref if whole else x_ref.at[k],
            dst_ref=out_ref.at[k],
            send_sem=send_sem.at[k],
            recv_sem=recv_sem.at[k],
            device_id=peer(mask),
            device_id_type=MESH,
        )

    barrier = pltpu.get_barrier_semaphore()
    each(
        lambda k, mask: pl.semaphore_signal(
            barrier, inc=1, device_id=peer(mask), device_id_type=MESH
        )
    )
    pl.semaphore_wait(barrier, count - 1)
    each(lambda k, mask: copy(k, mask).start())
    own = pltpu.make_async_copy(x_ref if whole else x_ref.at[0], out_ref.at[0], own_sem)
    own.start()
    own.wait()
    each(lambda k, mask: copy(k, mask).wait())


def exchange(array, number, name, masks=None, whole=True):
    sizes = (lax.axis_size("wide"), lax.axis_size("narrow"))
    count = sizes[0] * sizes[1] if masks is None else len(masks)
    shape = (count,) + array.shape if whole else array.shape
    return pl.pallas_call(
        functools.partial(exchange_kernel, masks, sizes, whole),
        out_shape=jax.ShapeDtypeStruct(shape, array.dtype),
        in_specs=[pl.BlockSpec(memory_space=pltpu.VMEM)],
        out_specs=pl.BlockSpec(memory_space=pltpu.VMEM),
        scratch_shapes=[
            pltpu.SemaphoreType.DMA((count,)),
            pltpu.SemaphoreType.DMA((count,)),
            pltpu.SemaphoreType.DMA,
        ],
        compiler_params=pltpu.CompilerParams(
            collective_id=number, has_side_effects=True, vmem_limit_bytes=32 * MIB
        ),
        name=name,
    )(array)


def merge_stats(stats):
    masks = group_masks()
    rows = stats.shape[1] // 4
    parts = exchange(stats, 1, "stats_swap", masks, False)
    top, total, picked = (parts[:, i * rows : (i + 1) * rows] for i in range(3))
    highest = jnp.max(top, 0)
    own = highest + jnp.log(jnp.sum(total * jnp.exp(top - highest), 0))
    share = exchange(jnp.pad(own, ((0, -rows % 8), (0, 0))), 8, "stats_share", masks)
    return share[:, :rows], own, jnp.sum(picked, 0)


def put_columns(rows_ref, column_ref):
    turned = rows_ref[...].T
    for place in range(rows_ref.shape[0]):
        column_ref[pl.ds(place * 128, 128), :] = turned[:, place : place + 1]


def as_rows(column):
    count = column.shape[0] // 128
    return jnp.concatenate(
        [column[place * 128 : (place + 1) * 128] for place in range(count)], 1
    ).T


def score_kernel(
    rows_ref, table_ref, target_ref, exps_ref, max_ref, stat_ref, sum_ref, pick_ref, column_ref
):
    tile = pl.program_id(0)
    width = table_ref.shape[0]

    @pl.when(tile == 0)
    def _():
        max_ref[...] = jnp.full_like(max_ref, -jnp.inf)
        sum_ref[...] = jnp.zeros_like(sum_ref)
        pick_ref[...] = jnp.zeros_like(pick_ref)
        put_columns(target_ref, column_ref)

    def step(block, carry):
        rows = pl.ds(pl.multiple_of(block * TOKEN_TILE, TOKEN_TILE), TOKEN_TILE)
        scores = lax.dot_general(
            rows_ref[rows, :],
            table_ref[...],
            (((1,), (1,)), ((), ())),
            preferred_element_type=jnp.float32,
        )
        top = jnp.max(scores, -1, keepdims=True)
        powers = jnp.exp(scores - top)
        exps_ref[rows, :] = powers.astype(jnp.bfloat16)
        total = jnp.sum(powers, -1, keepdims=True)
        columns = lax.broadcasted_iota(jnp.int32, (TOKEN_TILE, width), 1)
        wanted = column_ref[rows, :] - tile * width
        hit = jnp.sum(jnp.where(columns == wanted, scores, 0.0), -1, keepdims=True)
        here = lax.broadcasted_iota(jnp.int32, (TOKEN_TILE, 128), 1) == tile
        max_ref[rows, :] = jnp.where(here, top, max_ref[rows, :])
        sum_ref[rows, :] = jnp.where(here, total, sum_ref[rows, :])
        pick_ref[rows, :] = jnp.where(here, hit, pick_ref[rows, :])
        return carry

    lax.fori_loop(0, rows_ref.shape[0] // TOKEN_TILE, step, 0, unroll=8)

    @pl.when(tile == pl.num_programs(0) - 1)
    def _():
        maxima = max_ref[...]
        top = jnp.max(maxima, -1, keepdims=True)
        total = jnp.sum(sum_ref[...] * jnp.exp(maxima - top), -1, keepdims=True)
        picked = jnp.sum(pick_ref[...], -1, keepdims=True)
        blocks, height, _ = stat_ref.shape
        rows = height // 4
        stat_ref[...] = jnp.zeros_like(stat_ref)
        for number, column in enumerate((top, total, picked)):
            lines = as_rows(column)
            for block in range(blocks):
                stat_ref[block, pl.ds(number * rows, rows), :] = lines[
                    block * rows : (block + 1) * rows
                ]


def vocab_tile(vocab):
    return 1280 if vocab % 1280 == 0 else 640


def head_scores(rows, table, targets, blocks):
    tokens, model = rows.shape
    vocab = table.shape[0]
    width = vocab_tile(vocab)
    stat = pltpu.VMEM((tokens, 128), jnp.float32)
    whole = pl.BlockSpec((tokens, 128), lambda j: (0, 0))
    height = 4 * (tokens // blocks // 128)
    return pl.pallas_call(
        score_kernel,
        grid=(vocab // width,),
        out_shape=(
            jax.ShapeDtypeStruct((tokens, vocab), jnp.bfloat16),
            jax.ShapeDtypeStruct((tokens, 128), jnp.float32),
            jax.ShapeDtypeStruct((blocks, height, 128), jnp.float32),
        ),
        in_specs=[
            pl.BlockSpec((tokens, model), lambda j: (0, 0)),
            pl.BlockSpec((width, model), lambda j: (j, 0)),
            pl.BlockSpec(targets.shape, lambda j: (0, 0)),
        ],
        out_specs=(
            pl.BlockSpec((tokens, width), lambda j: (0, j)),
            whole,
            pl.BlockSpec((blocks, height, 128), lambda j: (0, 0, 0)),
        ),
        scratch_shapes=[stat, stat, pltpu.VMEM((tokens, 1), jnp.int32)],
        compiler_params=pltpu.CompilerParams(vmem_limit_bytes=60 * MIB),
        cost_estimate=pl.CostEstimate(
            flops=3 * tokens * vocab * model,
            bytes_accessed=2 * tokens * vocab,
            transcendentals=tokens * vocab,
        ),
        name="head_scores",
    )(rows, table, targets)


def slope_kernel(
    exps_ref,
    max_ref,
    log_ref,
    target_ref,
    table_ref,
    slope_ref,
    grad_ref,
    total_ref,
    column_ref,
    log_column_ref,
):
    tile = pl.program_id(0)
    width = table_ref.shape[0]

    @pl.when(tile == 0)
    def _():
        total_ref[...] = jnp.zeros_like(total_ref)
        put_columns(target_ref, column_ref)
        put_columns(log_ref, log_column_ref)

    def step(block, carry):
        rows = pl.ds(pl.multiple_of(block * TOKEN_TILE, TOKEN_TILE), TOKEN_TILE)
        here = lax.broadcasted_iota(jnp.int32, (TOKEN_TILE, 128), 1) == tile
        top = jnp.sum(jnp.where(here, max_ref[rows, :], 0.0), -1, keepdims=True)
        scale = jnp.exp(top - log_column_ref[rows, :])
        columns = lax.broadcasted_iota(jnp.int32, (TOKEN_TILE, width), 1)
        wanted = column_ref[rows, :] - tile * width
        probs = exps_ref[rows, :].astype(jnp.float32) * scale
        slope = jnp.where(columns == wanted, probs - 1.0, probs).astype(jnp.bfloat16)
        slope_ref[rows, :] = slope
        total_ref[rows, :] += jnp.dot(slope, table_ref[...], preferred_element_type=jnp.float32)
        return carry

    lax.fori_loop(0, exps_ref.shape[0] // TOKEN_TILE, step, 0, unroll=8)

    @pl.when(tile == pl.num_programs(0) - 1)
    def _():
        grad_ref[...] = total_ref[...].astype(jnp.bfloat16)


def head_slopes(exps, maxima, logs, targets, table):
    tokens, vocab = exps.shape
    model = table.shape[1]
    width = vocab_tile(vocab)
    return pl.pallas_call(
        slope_kernel,
        grid=(vocab // width,),
        out_shape=(
            jax.ShapeDtypeStruct((tokens, vocab), jnp.bfloat16),
            jax.ShapeDtypeStruct((tokens, model), jnp.bfloat16),
        ),
        in_specs=[
            pl.BlockSpec((tokens, width), lambda j: (0, j)),
            pl.BlockSpec((tokens, 128), lambda j: (0, 0)),
            pl.BlockSpec(logs.shape, lambda j: (0, 0)),
            pl.BlockSpec(targets.shape, lambda j: (0, 0)),
            pl.BlockSpec((width, model), lambda j: (j, 0)),
        ],
        out_specs=(
            pl.BlockSpec((tokens, width), lambda j: (0, j)),
            pl.BlockSpec((tokens, model), lambda j: (0, 0)),
        ),
        scratch_shapes=[
            pltpu.VMEM((tokens, model), jnp.float32),
            pltpu.VMEM((tokens, 1), jnp.int32),
            pltpu.VMEM((tokens, 1), jnp.float32),
        ],
        compiler_params=pltpu.CompilerParams(vmem_limit_bytes=60 * MIB),
        cost_estimate=pl.CostEstimate(
            flops=3 * tokens * vocab * model,
            bytes_accessed=4 * tokens * vocab,
            transcendentals=0,
        ),
        input_output_aliases={0: 0},
        name="head_slopes",
    )(exps, maxima, logs, targets, table)


def slots():
    wides, ups = chip_sizes()
    return 32 if wides * ups <= 16 else 16


def one_hot(places, size):
    return (places.reshape(-1, 1) == jnp.arange(size)[None]).astype(jnp.bfloat16)


def token_plan(ids_all, shard_rows):
    chips, tokens = ids_all.shape
    wides, ups = chip_sizes()
    wide, narrow = lax.axis_index("wide"), lax.axis_index("narrow")
    own_core = narrow % 2
    own_chip = wide * ups + narrow // 2
    owner = ids_all // shard_rows
    owner_core = jnp.bitwise_xor(owner % 2, own_core)
    owner_chip = jnp.bitwise_xor(owner // 2, own_chip)
    local = ids_all % shard_rows
    row = lax.broadcasted_iota(jnp.int32, (tokens, tokens), 0)
    column = lax.broadcasted_iota(jnp.int32, (tokens, tokens), 1)
    before = column < row
    alike = ids_all[:, :, None] == ids_all[:, None, :]
    first = ~jnp.any(alike & before[None], 2)
    served = first & (owner_chip == 0) & (owner_core == 0)
    served_rank = times_t(served.astype(jnp.bfloat16), before.astype(jnp.bfloat16)).astype(
        jnp.int32
    )
    half = tokens // 2
    mine = lambda array: lax.dynamic_slice_in_dim(array, own_core * half, half)
    own_first = mine(jnp.min(jnp.where(alike[0], column, tokens), 1))
    same_owner = mine(owner[0])[:, None] == owner[0][None]
    own_rank = jnp.sum(
        (same_owner & first[0][None] & (column[:half] < own_first[:, None])).astype(jnp.int32), 1
    )
    own_block = mine(owner_core[0]) * chips + mine(owner_chip[0])
    most = jnp.max(
        jnp.sum(
            (
                first[:, None, :]
                & (owner[:, None, :] == jnp.arange(2 * chips)[None, :, None])
            ).astype(jnp.int32),
            2,
        )
    )
    rounds = (most + slots() - 1) // slots()

    def plan(turn):
        slot = jnp.arange(slots())[None, :, None] + turn * slots()
        chosen = served[:, None, :] & (served_rank[:, None, :] == slot)
        slot_rows = jnp.sum(jnp.where(chosen, local[:, None, :] + 1, 0), 2) - 1
        inside = own_rank - turn * slots()
        valid = (inside >= 0) & (inside < slots())
        own_slots = jnp.where(valid, own_block * slots() + inside, -1)
        return slot_rows, one_hot(own_slots, 2 * chips * slots())

    return plan, rounds


def later_rounds(rounds, turn, total):
    return lax.while_loop(
        lambda state: state[0] < rounds,
        lambda state: (state[0] + 1, state[1] + turn(state[0])),
        (jnp.ones((), jnp.int32), total),
    )[1]


def norm_kernel(sizes, tile, table_ref, passed_ref, slot_ref, rows_ref, small_ref, matrix_ref, scalar_ref, *refs):
    total_ref, sum_ref, sent_ref, got_ref, send_sem, recv_sem = refs
    wides, groups = sizes
    place = Place(wides, groups)
    count = wides * groups
    barrier = pltpu.get_barrier_semaphore()
    for k in range(1, count):
        pl.semaphore_signal(
            barrier, inc=1, device_id=place.peer(k // groups, k % groups), device_id_type=MESH
        )
    width = table_ref.shape[1]

    def step(i, squares):
        span = pl.ds(pl.multiple_of(i * tile, 8), tile)
        row = lax.broadcasted_iota(jnp.int32, (tile, slot_ref.shape[1]), 0) + i * tile
        hot = (row == slot_ref[...]).astype(jnp.float32).astype(jnp.bfloat16)
        total = table_ref[span, :] + passed_ref[span, :].astype(jnp.float32)
        total = total + plain(hot, rows_ref[...])
        total_ref[span, :] = total
        return squares + jnp.sum((total * total).reshape(tile // 8, 8, width), 0)

    squares = lax.fori_loop(
        0, table_ref.shape[0] // tile, step, jnp.zeros((8, width), jnp.float32)
    )
    own = jnp.sum(squares + matrix_ref[...], keepdims=True)
    lane = lax.broadcasted_iota(jnp.int32, (8, 128), 1)
    sent_ref[...] = scalar_ref[...] + jnp.where(lane == 2, own, 0.0)
    pl.semaphore_wait(barrier, count - 1)

    def copy(k):
        return pltpu.make_async_remote_copy(
            src_ref=sent_ref,
            dst_ref=got_ref.at[k],
            send_sem=send_sem.at[k],
            recv_sem=recv_sem.at[k],
            device_id=place.peer(k // groups, k % groups),
            device_id_type=MESH,
        )

    for k in range(1, count):
        copy(k).start()
    got_ref[0] = sent_ref[...]
    small = small_ref[...]
    copied = jnp.sum(small * small, keepdims=True)
    for k in range(1, count):
        copy(k).wait()
    both = got_ref[...]
    total = jnp.zeros((8, 128), jnp.float32)
    order = device_order(place, wides, groups, both)
    for one in order:
        total = total + one
    sum_ref[...] = total + jnp.where(lane == 2, copied, 0.0)


def device_order(place, wides, groups, blocks):
    flat = [blocks[k] for k in range(wides * groups)]
    sides = [(groups << bit, place.wide // (1 << bit) % 2) for bit in range(log_two(wides))]
    sides += [(1 << bit, place.narrow // (1 << bit) % 2) for bit in range(log_two(groups))]
    for step, side in sides:
        one = side == 1
        flat = [jnp.where(one, flat[k ^ step], flat[k]) for k in range(len(flat))]
    return flat


def table_norm(table_sum, passed, slot_rows, rows, small, matrix_squares, scalars):
    sizes = (lax.axis_size("wide"), lax.axis_size("narrow"))
    count = sizes[0] * sizes[1]
    height, width = table_sum.shape
    tile = next(size for size in (400, 80, 16) if height % size == 0)
    vmem = pl.BlockSpec(memory_space=pltpu.VMEM)
    return pl.pallas_call(
        functools.partial(norm_kernel, sizes, tile),
        out_shape=(
            jax.ShapeDtypeStruct((height, width), jnp.float32),
            jax.ShapeDtypeStruct((8, 128), jnp.float32),
        ),
        in_specs=[vmem] * 7,
        out_specs=(vmem, vmem),
        scratch_shapes=[
            pltpu.VMEM((8, 128), jnp.float32),
            pltpu.VMEM((count, 8, 128), jnp.float32),
        ]
        + mail_sems(count),
        compiler_params=pltpu.CompilerParams(
            collective_id=3, has_side_effects=True, vmem_limit_bytes=62 * MIB
        ),
        name="table_norm",
    )(table_sum, passed, slot_rows.reshape(1, -1), rows, small, matrix_squares, scalars)


def upper_blocks(count):
    return [(i, j) for i in range(count) for j in range(i, count)]


def muon_kernel(lane_bits, *refs):
    core, _, y_bits, _ = lane_bits
    low_refs, factor_ref, table_refs = refs[:4], refs[4], refs[5:9]
    rest_out, size_out, table_outs = *refs[9:11], refs[11:14]
    gram, sent, got, back, full, total, half, low_a, low_b, low_c, send_sem, recv_sem = refs[14:26]
    in_tiles, out_tiles, in_sem, out_sem = refs[26:]
    width = full.shape[0]
    block = gram.shape[-1]
    places = upper_blocks(width // block)
    greet([neighbour(bit) for bit in [core] + y_bits])
    mail = Mail(send_sem, recv_sem, lane_bits)

    def adam_flow():
        tile = in_tiles.shape[2]
        count = table_refs[0].shape[0] // tile

        def loads(number):
            span = pl.ds(number * tile, tile)
            return [
                pltpu.make_async_copy(
                    ref.at[span], in_tiles.at[number % 2, kind], in_sem.at[number % 2, kind]
                )
                for kind, ref in enumerate(table_refs)
            ]

        def stores(number):
            span = pl.ds(number * tile, tile)
            return [
                pltpu.make_async_copy(
                    out_tiles.at[number % 2, kind], ref.at[span], out_sem.at[number % 2, kind]
                )
                for kind, ref in enumerate(table_outs)
            ]

        for copy in loads(0):
            copy.start()
        yield mail.now
        for number in range(count):
            if number + 1 < count:
                for copy in loads(number + 1):
                    copy.start()
            for copy in loads(number):
                copy.wait()
            if number >= 2:
                for copy in stores(number - 2):
                    copy.wait()
            weight, moment, square, grad = (in_tiles[number % 2, kind] for kind in range(4))
            results = adam_step(
                weight, moment, square, grad * factor_ref[0:1, 0:1], EMBED_RATE, DECAY
            )
            for kind, result in enumerate(results):
                out_tiles[number % 2, kind] = result
            for copy in stores(number):
                copy.start()
            yield mail.spend(1.2)
        for number in range(max(count - 2, 0), count):
            for copy in stores(number):
                copy.wait()

    mail.run([muon_flow(mail, lane_bits, refs, places), adam_flow()])
    mail.close()
    for number in range(4):

        def put_out(i, j, piece, number=number):
            rest_out[number, pl.ds(i * block, block), pl.ds(j * block, block)] = piece.astype(
                jnp.bfloat16
            )

        unpack(places, lambda place: back[number, place].astype(jnp.float32), put_out)


def unpack(places, source, target):
    for place, (i, j) in enumerate(places):
        piece = source(place)
        target(i, j, piece)
        if i != j:
            target(j, i, piece.T)


def muon_flow(mail, lane_bits, refs, places):
    core, _, y_bits, _ = lane_bits
    low_refs, size_out = refs[:4], refs[10]
    gram, sent, got, back, full, total, half, low_a, low_b, low_c = refs[14:24]
    width = full.shape[0]
    block = gram.shape[-1]
    narrow = lax.axis_index("narrow")
    own_core, own_up = narrow % 2, (narrow // 2) % 2
    own = 2 * own_core + own_up
    for number, low_ref in enumerate(low_refs):
        for place, (i, j) in enumerate(places):
            product = lax.dot_general(
                low_ref[:, i * block : (i + 1) * block],
                low_ref[:, j * block : (j + 1) * block],
                (((0,), (0,)), ((), ())),
                preferred_element_type=jnp.float32,
            )
            gram[number, place] = product
    for slot in range(2):
        sent[slot] = gram[2 * (1 - own_core) + slot].astype(jnp.bfloat16)
    copy = mail.post(sent.at[pl.ds(0, 2)], got.at[pl.ds(0, 2)], core)
    yield mail.due
    mail.take(copy)

    def add(number, slot):
        for place in range(len(places)):
            gram[number, place] += got[slot, place].astype(jnp.float32)

    def pass_on(number, slot, bit):
        sent[slot] = gram[number].astype(jnp.bfloat16)
        return mail.post(sent.at[slot], got.at[slot], bit)

    other_up = 2 * own_core + 1 - own_up
    if y_bits:
        add(other_up, 1 - own_up)
        over_y = pass_on(other_up, 2, y_bits[0])
        add(own, own_up)
        yield mail.due
        mail.take(over_y)
        add(own, 2)
    for level, bit in enumerate(y_bits[1:]):
        copy = pass_on(own, 3 + level, bit)
        yield mail.due
        mail.take(copy)
        add(own, 3 + level)

    def spans(i, j):
        return pl.ds(i * block, block), pl.ds(j * block, block)

    def put_full(i, j, piece):
        full[spans(i, j)] = piece

    unpack(places, lambda place: gram[own, place], put_full)
    diagonal = lax.broadcasted_iota(jnp.int32, (block, block), 0) == lax.broadcasted_iota(
        jnp.int32, (block, block), 1
    )
    trace = jnp.zeros((1, 1), jnp.float32)
    for i in range(width // block):
        trace = trace + jnp.sum(jnp.where(diagonal, full[spans(i, i)], 0.0), keepdims=True)
    magnitude = jnp.sqrt(trace) + 1e-07
    inverse = 1.0 / magnitude

    def rows(step):
        def body(i, carry):
            step(pl.ds(pl.multiple_of(i * block, block), block))
            return carry

        lax.fori_loop(0, width // block, body, 0)

    def times(left, right, span):
        return jnp.dot(left[span, :], right[...], preferred_element_type=jnp.float32)

    def start(span):
        scaled = full[span, :] * (inverse * inverse)
        full[span, :] = scaled
        low_a[span, :] = scaled.astype(jnp.bfloat16)

    rows(start)
    scale = NS_A
    for cycle_no in range(NS_STEPS):

        def rest_step(span):
            rest = NS_B * full[span, :] + NS_C * times(low_a, low_a, span)
            low_b[span, :] = rest.astype(jnp.bfloat16)
            if cycle_no == 0:
                total[span, :] = rest
            else:
                total[span, :] = NS_A * total[span, :] + scale * rest

        rows(rest_step)
        if cycle_no:

            def total_step(span):
                total[span, :] += times(low_c, low_b, span)

            rows(total_step)
            scale = scale * NS_A
        if cycle_no < NS_STEPS - 1:

            def keep_total(span):
                low_c[span, :] = total[span, :].astype(jnp.bfloat16)

            def half_step(span):
                half[span, :] = NS_A * full[span, :] + times(low_a, low_b, span)

            def full_step(span):
                value = half[span, :]
                low_a[span, :] = value.astype(jnp.bfloat16)
                full[span, :] = NS_A * value + times(low_a, low_b, span)

            def low_step(span):
                low_a[span, :] = full[span, :].astype(jnp.bfloat16)

            rows(keep_total)
            rows(half_step)
            rows(full_step)
            rows(low_step)

    for place, (i, j) in enumerate(places):
        back[own, place] = (total[spans(i, j)] * inverse).astype(jnp.bfloat16)
    lane = lax.broadcasted_iota(jnp.int32, (8, 128), 1)
    size_out[own] = jnp.where(lane >= 0, inverse, 0.0)
    mail.post(back.at[own], back.at[own], core)
    mail.post(size_out.at[own], size_out.at[own], core)
    if y_bits:
        over_size = mail.post(size_out.at[own], size_out.at[own], y_bits[0])
        over_y = mail.post(back.at[own], back.at[own], y_bits[0])
        yield mail.due
        mail.take(over_y)
        mail.take(over_size)
        mail.post(back.at[other_up], back.at[other_up], core)
        mail.post(size_out.at[other_up], size_out.at[other_up], core)


def muon_factors(lows, factor, table):
    width = lows[0].shape[1]
    block = 256
    count = len(upper_blocks(width // block))
    lane_bits = lanes()
    extra = max(len(lane_bits[2]) - 1, 0)
    vmem = pl.BlockSpec(memory_space=pltpu.VMEM)
    square = (width, width)
    height = table[0].shape[0]
    tile = next(size for size in (160, 80, 40, 16, 8) if height % size == 0)
    any_space = pl.BlockSpec(memory_space=pl.ANY)
    whole = jax.ShapeDtypeStruct(table[0].shape, jnp.float32)
    rests, sizes, *table_next = pl.pallas_call(
        functools.partial(muon_kernel, lane_bits),
        out_shape=(
            jax.ShapeDtypeStruct((4,) + square, jnp.bfloat16),
            jax.ShapeDtypeStruct((4, 8, 128), jnp.float32),
            whole,
            whole,
            whole,
        ),
        in_specs=[vmem] * 5 + [any_space] * 4,
        out_specs=(vmem, vmem, any_space, any_space, any_space),
        scratch_shapes=[
            pltpu.VMEM((4, count, block, block), jnp.float32),
            pltpu.VMEM((3 + extra, count, block, block), jnp.bfloat16),
            pltpu.VMEM((3 + extra, count, block, block), jnp.bfloat16),
            pltpu.VMEM((4, count, block, block), jnp.bfloat16),
        ]
        + [pltpu.VMEM(square, jnp.float32) for _ in range(3)]
        + [pltpu.VMEM(square, jnp.bfloat16) for _ in range(3)]
        + mail_sems(32)
        + [
            pltpu.VMEM((2, 4, tile, width), jnp.float32),
            pltpu.VMEM((2, 3, tile, width), jnp.float32),
            pltpu.SemaphoreType.DMA((2, 4)),
            pltpu.SemaphoreType.DMA((2, 3)),
        ],
        compiler_params=pltpu.CompilerParams(
            collective_id=9, has_side_effects=True, vmem_limit_bytes=56 * MIB
        ),
        name="muon_factors",
    )(*lows, jnp.full((8, 128), factor), *table)
    return rests, sizes[:, 0, 0], table_next


def on_device(
    token_ids,
    targets,
    joint_weight,
    output_weight,
    expand_weight,
    reduce_weight,
    joint_velocity,
    output_velocity,
    expand_velocity,
    reduce_velocity,
    embedding,
    embed_moment,
    embed_square,
    positions,
    position_moment,
    position_square,
    norm_gains,
    gain_moment,
    gain_square,
    biases,
    bias_moment,
    bias_square,
):
    core, x_bits, y_bits, z_bits = lanes()
    groups = lax.axis_size("narrow")
    wides = lax.axis_size("wide")
    across = 1 << len(x_bits)
    model_width = embedding.shape[1]
    shard_rows = embedding.shape[0]
    tokens = token_ids.shape[0] * LENGTH
    bias_rows = biases.reshape(-1, model_width)

    own_rows = embedding.astype(jnp.bfloat16)
    labels = jnp.concatenate([token_ids.reshape(-1, 128), targets.reshape(-1, 128)])
    spare = -labels.shape[0] % 8
    labels = exchange(jnp.pad(labels, ((0, spare), (0, 0))), 0, "label_share")
    ids_all = labels[:, : tokens // 128].reshape(-1, tokens)
    lines = tokens // 128
    own_block = lax.axis_index("wide") * groups + lax.axis_index("narrow")
    wides, ups = chip_sizes()
    pairs = ids_all.reshape(wides, ups, 2, tokens)
    other_first = lax.axis_index("narrow") % 2 == 1
    ids_chips = jnp.where(other_first, lax.rev(pairs, (2,)), pairs).reshape(wides * ups, -1)
    plan, rounds = token_plan(ids_chips, shard_rows)

    def serve(slot_rows):
        served = one_hot(slot_rows, shard_rows)
        return plain(served, own_rows).astype(jnp.bfloat16).reshape(-1, slots(), model_width)

    masters = (joint_weight, output_weight, expand_weight, reduce_weight)
    served, wanted = plan(0)
    table, weights, token_rows = load_all(
        own_rows, [master.astype(jnp.bfloat16) for master in masters], serve(served)
    )
    vocab_here = table.shape[0]

    def fetch(turn):
        more, places = plan(turn)
        got = swap_rows(serve(more))
        return plain(places, jnp.stack([got, swap(got, core)]).reshape(-1, model_width))

    embedded = later_rounds(rounds, fetch, plain(wanted, token_rows.reshape(-1, model_width)))

    block_masks = jnp.array(group_masks())
    targets_group = labels[block_masks, lines : 2 * lines].reshape(-1, 128)
    table_mask = groups * (across - 1) + 1
    differ = jnp.bitwise_xor(targets_group // shard_rows, own_block)
    is_owned = (targets_group >= 0) & (jnp.bitwise_and(differ, ~table_mask) == 0)
    place = (differ % 2) * across + (differ // groups) % across
    rows_targets = jnp.where(is_owned, place * shard_rows + targets_group % shard_rows, -1)
    final_low, *saved = layer_forward(embedded, positions, norm_gains, bias_rows, weights)
    group_rows = spread(final_low).reshape(-1, model_width)
    blocks = len(group_masks())
    exps, maxima, stats = head_scores(group_rows, table, rows_targets, blocks)
    logs, own_logs, own_picked = merge_stats(stats)
    loss_part = jnp.sum(
        jnp.where(targets.reshape(-1, 128) >= 0, own_logs - own_picked, 0.0)
    )
    logs = jnp.where(targets_group >= 0, logs.reshape(-1, 128), jnp.inf)
    slopes, final_part = head_slopes(exps, maxima, logs, rows_targets, table)
    final_grad, table_sum, passed = head_back(
        final_part.reshape(-1, tokens, model_width), slopes, group_rows
    )
    for bit in reversed(x_bits):
        passed = swap(passed, bit)
        if bit != x_bits[0]:
            table_sum = table_sum + passed.astype(jnp.float32)
            half = table_sum.shape[0] // 2
            table_sum, passed = table_sum[:half], table_sum[half:].astype(jnp.bfloat16)
    (front, expand_sum, reduce_sum), small, row_sums, squares, low_grad = back_reduce(
        final_grad, norm_gains, bias_rows, saved, weights, wanted
    )
    count_part = jnp.sum((targets >= 0).astype(jnp.float32))

    def bundle(places):
        both = outer_sum(places, low_grad).astype(jnp.bfloat16)
        both = both.reshape(2, -1, slots(), model_width)
        other = swap(both[1], core)
        return (both[0].astype(jnp.float32) + other.astype(jnp.float32)).astype(jnp.bfloat16)

    joint_rows = joint_weight.shape[0]
    def give(turn):
        more, places = plan(turn)
        got = swap_rows(bundle(places)).reshape(-1, model_width)
        return outer_sum(one_hot(more, shard_rows), got)

    table_sum = later_rounds(rounds, give, table_sum)
    places = jnp.stack([loss_part, count_part]).reshape(1, 2)
    table_sum, scalars = table_norm(
        table_sum,
        passed,
        served,
        row_sums.reshape(-1, model_width),
        small,
        squares,
        jnp.pad(places, ((0, 7), (0, 126))),
    )
    matrix_total = [
        part.astype(jnp.float32)
        for part in (front[:joint_rows], front[joint_rows:], expand_sum, reduce_sum)
    ]
    small = small[: 14 + LENGTH]
    loss_sum, loss_count, squares = scalars[0, 0], scalars[0, 1], scalars[0, 2]
    gain_grad, position_grad = small[:3], small[14:]
    bias_grad = small[3:14].reshape(-1)
    grad_norm = jnp.sqrt(squares) / loss_count
    factor = jnp.minimum(1.0, CLIP / (grad_norm + 1e-06)) / loss_count
    previous = (joint_velocity, output_velocity, expand_velocity, reduce_velocity)
    carried = tuple(
        (MOMENTUM * before + gradient * factor for before, gradient in zip(previous, matrix_total))
    )
    lows = [moment.astype(jnp.bfloat16) for moment in carried]
    rests, inverses, table_out = muon_factors(
        lows, factor, (embedding, embed_moment, embed_square, table_sum)
    )
    updated = []
    for number, (master, moment) in enumerate(zip(masters, carried)):
        orth = moment * (NS_A**NS_STEPS * inverses[number]) + plain(
            lows[number], rests[number]
        )
        shape_factor = math.sqrt(max(1.0, master.shape[0] * groups / master.shape[1]))
        updated.append(master * (1 - MUON_RATE * DECAY) - MUON_RATE * shape_factor * orth)
    place_out = adam_step(
        positions, position_moment, position_square, position_grad * factor, PLACE_RATE, DECAY
    )
    gain_out = adam_step(norm_gains, gain_moment, gain_square, gain_grad * factor, SMALL_RATE, 0.0)
    bias_out = adam_step(biases, bias_moment, bias_square, bias_grad * factor, SMALL_RATE, 0.0)
    return (
        loss_sum,
        loss_count,
        grad_norm,
        updated[0],
        updated[1],
        updated[2],
        updated[3],
        carried[0],
        carried[1],
        carried[2],
        carried[3],
        table_out[0],
        table_out[1],
        table_out[2],
        place_out[0],
        place_out[1],
        place_out[2],
        gain_out[0],
        gain_out[1],
        gain_out[2],
        bias_out[0],
        bias_out[1],
        bias_out[2],
    )


def solution(mesh):
    in_specs = (
        P(("wide", "narrow"), None),
        P(("wide", "narrow"), None),
        P("narrow", None),
        P("narrow", None),
        P("narrow", None),
        P("narrow", None),
        P("narrow", None),
        P("narrow", None),
        P("narrow", None),
        P("narrow", None),
        P(("wide", "narrow"), None),
        P(("wide", "narrow"), None),
        P(("wide", "narrow"), None),
        P(),
        P(),
        P(),
        P(),
        P(),
        P(),
        P(),
        P(),
        P(),
    )
    out_specs = (
        P(),
        P(),
        P(),
        P("narrow", None),
        P("narrow", None),
        P("narrow", None),
        P("narrow", None),
        P("narrow", None),
        P("narrow", None),
        P("narrow", None),
        P("narrow", None),
        P(("wide", "narrow"), None),
        P(("wide", "narrow"), None),
        P(("wide", "narrow"), None),
        P(),
        P(),
        P(),
        P(),
        P(),
        P(),
        P(),
        P(),
        P(),
    )
    return jax.shard_map(
        on_device, mesh=mesh, in_specs=in_specs, out_specs=out_specs, check_vma=False
    )
```

profile of v0, /device:TPU:0, one launch (start us, length us, event | category | flops | bytes accessed | tf_op | source)
XLA Modules:
  0.0 585.7 jit_solution(14028997225427842862)
XLA Ops:
  2.3 11.5 %label_share.1 = s32[32,8,128]{2,1,0:T(8,128)S(1)} custom-call(s32[8,128]{1,0:T(8,128)S(1)} %pad.13.x_ref), custom_call_target="tpu_custom_call" | custom-call | tf_op jit(solution)/shard_map/label_share/pallas_call | solution.py:1156
  14.2 6.2 %broadcast_compare_fusion = (pred[16,512,512]{2,1,0:T(8,128)(4,1)}, pred[16,512]{1,0:T(8,128)(4,1)S(1)}) fusion(s32[16,512]{1,0:T(8,128)S(1)} %bitcast.110, pred[512,512]{1,0:T(8,128)(4,1)S(1)} %iota_compare_fusion.18), kind=kLoop, calls=%fused_computation.28 | loop fusion | flops 12574720 | bytes 4497408 | tf_op jit(solution)/shard_map/eq | solution.py:1391
  23.4 4.2 convert_element_type.99.refs_0_
  33.8 4.3 fusion.9
  38.4 77.7 %load_rows.1 = (bf16[2,2,1600,768]{3,2,1,0:T(8,128)(2,1)}, bf16[4,576,768]{2,1,0:T(8,128)(2,1)}, bf16[4,192,768]{2,1,0:T(8,128)(2,1)}, bf16[4,768,768]{2,1,0:T(8...) custom-call(bf16[1600,768]{1,0:T(8,128)(2,1)} %convert_element_type.99.refs_0_, ...), custom_call_target="tpu_custom_call" | custom-call | tf_op jit(solution)/shard_map/load_rows/pallas_call | solution.py:858
  118.5 12.2 %layer_forward.1 = (bf16[256,768]{1,0:T(8,128)(2,1)}, f32[3,256,768]{2,1,0:T(8,128)}, f32[3,256,128]{2,1,0:T(8,128)}, bf16[256,2304]{1,0:T(8,128)(2,1)}, bf16[256,768]{1,0:T(8,128)(2,1)}, /*index=5*/f32[256,3072]{1,0:T(8,128)}) custom-call(f32[256,768]{1,0:T(8,128)S(1)} %get-tuple-element.290.x_ref, f32[64,768]{1,0:T(8,128)} %place_ref.1, f32[3,768]{1,0:T(4,128)} %refs_1_.1, ...), custom_call_target="tpu_custom_call" | custom-call | tf_op jit(solution)/shard_map/layer_forward/pallas_call | solution.py:174
  130.6 39.5 %rows_spread.1 = bf16[8,256,768]{2,1,0:T(8,128)(2,1)} custom-call(bf16[256,768]{1,0:T(8,128)(2,1)} %get-tuple-element.295.x_ref), custom_call_target="tpu_custom_call" | custom-call | tf_op jit(solution)/shard_map/rows_spread/pallas_call | solution.py:521
  170.9 35.7 %head_scores.1 = (bf16[2048,6400]{1,0:T(8,128)(2,1)}, f32[2048,128]{1,0:T(8,128)}, f32[8,8,128]{2,1,0:T(8,128)}) custom-call(bf16[2048,768]{1,0:T(8,128)(2,1)} %bitcast.100, bf16[6400,768]{1,0:T(8,128)(2,1)} %bitcast.122, s32[16,128]{1,0:T(8,128)} %fusion.39.target_ref), custom_call_target="tpu_custom_call" | custom-call | flops 30198988800 | bytes 26214400 | tf_op jit(solution)/shard_map/head_scores/pallas_call | solution.py:1261
  207.3 6.7 %stats_swap.1 = f32[8,8,128]{2,1,0:T(8,128)S(1)} custom-call(f32[8,8,128]{2,1,0:T(8,128)S(1)} %copy-done), custom_call_target="tpu_custom_call" | custom-call | tf_op jit(solution)/shard_map/stats_swap/pallas_call | solution.py:1156
  214.1 6.8 %stats_share.1 = f32[8,8,128]{2,1,0:T(8,128)S(1)} custom-call(f32[8,128]{1,0:T(8,128)S(1)} %pad.14.x_ref), custom_call_target="tpu_custom_call" | custom-call | tf_op jit(solution)/shard_map/stats_share/pallas_call | solution.py:1156
  221.5 32.9 %head_slopes.1 = (bf16[2048,6400]{1,0:T(8,128)(2,1)}, bf16[2048,768]{1,0:T(8,128)(2,1)}) custom-call(bf16[2048,6400]{1,0:T(8,128)(2,1)} %get-tuple-element.297.exps_ref, f32[2048,128]{1,0:T(8,128)} %get-tuple-element.298.max_ref, f32[16,128]{1,0:T(8,128)} %broadcast_select_fusion.1.log_ref, ...), custom_call_target="tpu_custom_call", output_to_operand_aliasing={{0}: (0, {})} | custom-call | flops 30198988800 | bytes 52428800 | tf_op jit(solution)/shard_map/head_slopes/pallas_call | solution.py:1335
  254.4 47.5 %head_back.1 = (f32[256,768]{1,0:T(8,128)}, f32[1600,768]{1,0:T(8,128)}, bf16[1600,768]{1,0:T(8,128)(2,1)}) custom-call(bf16[8,256,768]{2,1,0:T(8,128)(2,1)} %bitcast.108, bf16[2048,6400]{1,0:T(8,128)(2,1)} %get-tuple-element.301.refs_0_, bf16[2048,768]{1,0:T(8,128)(2,1)} %bitcast.101), custom_call_target="tpu_custom_call" | custom-call | tf_op jit(solution)/shard_map/head_back/pallas_call | solution.py:651
  307.7 149.2 %back_reduce.1 = (bf16[768,768]{1,0:T(8,128)(2,1)}, bf16[768,768]{1,0:T(8,128)(2,1)}, bf16[768,768]{1,0:T(8,128)(2,1)}, f32[80,768]{1,0:T(8,128)}, bf16[16,32,76...) custom-call(f32[256,768]{1,0:T(8,128)} %get-tuple-element.303.refs_0_, f32[3,768]{1,0:T(4,128)} %refs_1_.1, ...), custom_call_target="tpu_custom_call" | custom-call | tf_op jit(solution)/shard_map/back_reduce/pallas_call | solution.py:1063
  456.9 15.7 %table_norm.1 = (f32[1600,768]{1,0:T(8,128)}, f32[8,128]{1,0:T(8,128)}) custom-call(f32[1600,768]{1,0:T(8,128)} %get-tuple-element.310.table_ref, bf16[1600,768]{1,0:T(8,128)(2,1)} %collective-permute-done.2.passed_ref, s32[1,512]{1,0:T(1,128)} %sub.120.slot_ref, bf16[512,768]{1,0:T(8,128)(2,1)} %bitcast.112, f32[80,768]{1,0:T(8,128)} %get-tuple-element.313.small_ref, ...), custom_call_target="tpu_custom_call" | custom-call | tf_op jit(solution)/shard_map/table_norm/pallas_call | solution.py:1506
  476.7 3.1 fusion.51
  484.3 2.2 fusion.48
  487.1 68.7 %muon_factors.1 = (bf16[4,768,768]{2,1,0:T(8,128)(2,1)}, f32[4,8,128]{2,1,0:T(8,128)}, f32[1600,768]{1,0:T(8,128)}, f32[1600,768]{1,0:T(8,128)}, f32[1600,768]{1,0:T(8,128)}) custom-call(bf16[576,768]{1,0:T(8,128)(2,1)} %get-tuple-element.380.refs_0_, bf16[192,768]{1,0:T(8,128)(2,1)} %get-tuple-element.378.refs_1_, ...), custom_call_target="tpu_custom_call" | custom-call | tf_op jit(solution)/shard_map/muon_factors/pallas_call | solution.py:1755
  560.2 4.7 multiply_subtract_fusion
  564.9 2.6 fusion.11
  567.5 2.6 add_subtract_fusion.1
  571.2 2.6 add_subtract_fusion
  576.0 2.5 copy.79
  578.5 2.4 copy.80
  581.9 2.2 copy.81
  (151 shorter events, 33.9 us)
Async XLA Ops:
  14.2 8.6 %copy-start.32 = (s32[8]{0:T(128)S(1)}, s32[8]{0:T(128)}, u32[]{:S(2)}) copy-start(s32[8]{0:T(128)} %constant.305) | copy-start | bytes 100
  23.4 4.2 copy-start.10
  23.4 5.2 copy-start.16
  254.4 50.7 %copy-start.35 = (s32[4,64]{1,0:T(4,128)S(1)}, s32[4,64]{1,0:T(4,128)}, u32[]{:S(2)}) copy-start(s32[4,64]{1,0:T(4,128)} %param.28) | copy-start | bytes 3076
  301.9 155.0 %collective-permute-start.2 = (bf16[1600,768]{1,0:T(8,128)(2,1)}, bf16[1600,768]{1,0:T(8,128)(2,1)}, u32[]{:S(2)}, u32[]{:S(2)}) collective-permute-start(bf16[1600,768]{1,0:T(8,128)(2,1)} %get-tuple-element.311), channel_id=1, source_target_pairs={{0,4},{4,0},{8,12},{12,8},{16,20},{20,16},{24,28},{28,24},{1,5},{5... | collective-permute-start | bytes 7372808 | tf_op jit(solution)/shard_map/ppermute | solution.py:347
  456.9 19.2 %copy-start.20 = (f32[80,768]{1,0:T(8,128)S(1)}, f32[80,768]{1,0:T(8,128)}, u32[]{:S(2)}) copy-start(f32[80,768]{1,0:T(8,128)} %get-tuple-element.313.small_ref) | copy-start | bytes 737284
  456.9 19.8 %copy-start.17 = (f32[576,768]{1,0:T(8,128)S(1)}, f32[576,768]{1,0:T(8,128)}, u32[]{:S(2)}) copy-start(f32[576,768]{1,0:T(8,128)} %param.33) | copy-start | bytes 5308420
  476.7 5.1 copy-start.14
  476.7 5.1 copy-start.19
  483.2 84.2 %copy-start.3 = (f32[768,768]{1,0:T(8,128)}, f32[768,768]{1,0:T(8,128)S(1)}, u32[]{:S(2)}) copy-start(f32[768,768]{1,0:T(8,128)S(1)} %get-tuple-element.624) | copy-start | bytes 7077892
  487.1 72.5 %copy-start.25 = (f32[11,768]{1,0:T(8,128)S(1)}, f32[11,768]{1,0:T(8,128)}, u32[]{:S(2)}) copy-start(f32[11,768]{1,0:T(8,128)} %slice_multiply_fusion.1) | copy-start | bytes 101380
  487.1 73.1 %copy-start.9 = (bf16[576,768]{1,0:T(8,128)(2,1)S(1)}, bf16[576,768]{1,0:T(8,128)(2,1)}, u32[]{:S(2)}) copy-start(bf16[576,768]{1,0:T(8,128)(2,1)} %get-tuple-element.380.refs_0_) | copy-start | bytes 2654212
  560.2 4.7 copy-start.12
  560.2 4.7 copy-start.13
  560.2 7.3 %copy-start.6 = (f32[768,768]{1,0:T(8,128)S(1)}, f32[768,768]{1,0:T(8,128)}, u32[]{:S(2)}) copy-start(f32[768,768]{1,0:T(8,128)} %param.31) | copy-start | bytes 7077892
  567.5 6.3 %copy-start.23 = (f32[64,768]{1,0:T(8,128)S(1)}, f32[64,768]{1,0:T(8,128)}, u32[]{:S(2)}) copy-start(f32[64,768]{1,0:T(8,128)} %param.41) | copy-start | bytes 589828
  567.5 6.3 %copy-start.24 = (f32[64,768]{1,0:T(8,128)S(1)}, f32[64,768]{1,0:T(8,128)}, u32[]{:S(2)}) copy-start(f32[64,768]{1,0:T(8,128)} %param.42) | copy-start | bytes 589828
  571.1 4.3 copy-start.27
  571.1 4.2 copy-start.28
  571.1 4.2 copy-start.30
  571.1 4.9 copy-start.11
  571.2 7.4 %slice-start.2 = ((s8[4915200]{0:T(1024)(128)(4,1)}), s8[4194304]{0:T(1024)(128)(4,1)S(1)}, s32[]{:S(2)}) async-start(s8[4915200]{0:T(1024)(128)(4,1)} %bitcast.104), calls=%async_computation.2 | async-start | bytes 8388608
  573.8 4.8 slice-start.3
  576.0 5.1 slice-start
  (17 other events, 47.6 us)
where the time goes:
time: 595 us; the launch traced here: 586 us
  Pallas kernels  504 us (85%)
  other arithmetic  33.1 us (6%)
  local copies, waits for them, and re-layouts  19.7 us (3%)
  matrix products  19 us (3%)
  between operations  8.19 us (1%)
    pallas_call x1, Pallas kernels, back_reduce(): pl.pallas_call(functools.partial(back_reduce_kernel, sizes, lane_bits, ki...  149 us
    pallas_call x1, Pallas kernels, load_all(): pl.pallas_call(functools.partial(load_kernel, sizes, lane_bits), out_shap...  77.7 us
    pallas_call x1, Pallas kernels, muon_factors(): pl.pallas_call(functools.partial(muon_kernel, lane_bits), out_shape=(jax....  68.7 us
    pallas_call x1, Pallas kernels, head_back(): pl.pallas_call(functools.partial(head_back_kernel, lane_bits, plan, tile)...  47.5 us
    pallas_call x1, Pallas kernels, spread(): pl.pallas_call(functools.partial(spread_kernel, lanes(), plan), out_shape...  39.5 us
    pallas_call x1, Pallas kernels, head_scores(): pl.pallas_call(score_kernel, grid=(vocab // width,), out_shape=(jax.Shape...  35.7 us
    pallas_call x1, Pallas kernels, head_slopes(): pl.pallas_call(slope_kernel, grid=(vocab // width,), out_shape=(jax.Shape...  32.9 us
    pallas_call x3, Pallas kernels, exchange(): pl.pallas_call(functools.partial(exchange_kernel, masks, sizes, whole), o...  25 us
  transfers between devices with their start and end apart: 1, of which 0 were waited for; matrix products, arithmetic and copies ran while one was open for 1% of the time, Pallas kernels for 25%

commit v1 on v0

--- a/solution.py
+++ b/solution.py
@@ -506,29 +506,45 @@
         yield mail.due
 
 
-def spread_kernel(lane_bits, plan, x_ref, out_ref, send_sem, recv_sem):
-    bits = lane_bits[3] + lane_bits[2]
-    greet([neighbour(bit) for bit in bits])
+def spread_kernel(lane_bits, plan, x_ref, *refs):
+    core, x_bits, y_bits, z_bits = lane_bits
+    count = 1 << len(x_bits)
+    table_refs, out_ref, table_out, send_sem, recv_sem = refs[:count], *refs[count:]
+    bits = z_bits + y_bits
+    greet([neighbour(bit) for bit in bits + [core]])
     mail = Mail(send_sem, recv_sem, lane_bits)
-    mail.run([spread_flow(mail, bits, part, x_ref, out_ref) for part in plan])
+
+    def table_flow():
+        yield 1.0
+        for place, ref in enumerate(table_refs):
+            mail.post(ref, table_out.at[1, place], core)
+            mail.keep(ref, table_out.at[0, place])
+
+    mail.run([spread_flow(mail, bits, part, x_ref, out_ref) for part in plan] + [table_flow()])
     mail.keep(x_ref, out_ref.at[0])
     mail.close()
 
 
-def spread(array):
+def spread(array, tables):
     bits, plan = group_bits(), routes(array.shape[0], SPREAD_ORDERS)
     count = 1 << len(bits)
-    return pl.pallas_call(
+    vmem, any_space = pl.BlockSpec(memory_space=pltpu.VMEM), pl.BlockSpec(memory_space=pl.ANY)
+    blocks, table = pl.pallas_call(
         functools.partial(spread_kernel, lanes(), plan),
-        out_shape=jax.ShapeDtypeStruct((count,) + array.shape, array.dtype),
-        in_specs=[pl.BlockSpec(memory_space=pltpu.VMEM)],
-        out_specs=pl.BlockSpec(memory_space=pl.ANY),
-        scratch_shapes=mail_sems(len(plan) * count),
+        out_shape=(
+            jax.ShapeDtypeStruct((count,) + array.shape, array.dtype),
+            jax.ShapeDtypeStruct((2, len(tables)) + tables[0].shape, array.dtype),
+        ),
+        in_specs=[vmem] * (1 + len(tables)),
+        out_specs=(any_space, any_space),
+        scratch_shapes=mail_sems(len(plan) * count + 2 * len(tables)),
         compiler_params=pltpu.CompilerParams(
             collective_id=4, has_side_effects=True, vmem_limit_bytes=62 * MIB
         ),
         name="rows_spread",
-    )(array)
+    )(array, *tables)
+    width = array.shape[1]
+    return blocks.reshape(-1, width), table.reshape(-1, width)
 
 
 def collect_flow(mail, bits, part, refs):
@@ -748,69 +764,71 @@
 def load_kernel(sizes, lane_bits, *refs):
     core, x_bits, y_bits, z_bits = lane_bits
     near = z_bits[0]
-    table_ref, weight_refs, rows_ref = refs[0], refs[1:5], refs[5]
-    table_out, weight_outs, rows_out = refs[6], refs[7:11], refs[11]
-    send_sem, recv_sem, rows_send, rows_recv, pass_send, pass_recv = refs[12:]
+    weight_refs, rows_ref = refs[:4], refs[4]
+    weight_outs, rows_out = refs[5:9], refs[9]
+    send_sem, recv_sem, rows_send, rows_recv, pass_send, pass_recv = refs[10:]
     wide, narrow = lax.axis_index("wide"), lax.axis_index("narrow")
     rows = Rows(sizes, rows_ref, rows_out.at[0], rows_send, rows_recv)
     rows.greet([neighbour(core)])
     mail = Mail(send_sem, recv_sem, lane_bits)
     side_near = (wide // near[1]) % 2
 
-    def part(ref, number, half):
-        count = ref.shape[1] // 2
-        return ref.at[number, pl.ds(pl.multiple_of(half * count, 16), count)]
-
-    def own_part(ref, half):
-        count = ref.shape[0] // 2
-        return ref.at[pl.ds(pl.multiple_of(half * count, 16), count)]
-
-    tables = {0: mail.keep(table_ref, table_out.at[0, 0])}
-    if x_bits:
-        tables[1] = mail.post(table_ref, table_out.at[0, 1], x_bits[0])
-    held = [0]
-    first = []
-    for ref, out in zip(weight_refs, weight_outs):
-        if y_bits:
-            first.append(
-                mail.post(own_part(ref, side_near), part(out, narrow, side_near), y_bits[0])
-            )
+    def across(block, bit):
+        return block + bit[1] * (1 - 2 * ((block // bit[1]) % 2))
+
+    def pieces(height):
+        half = height // 2
+        count = 2 if height == weight_refs[3].shape[0] and half % 32 == 0 else 1
+        return [(place * (half // count), half // count) for place in range(count)]
+
+    def part(ref, number, side, piece):
+        start = side * (ref.shape[1] // 2) + piece[0]
+        return ref.at[number, pl.ds(pl.multiple_of(start, 16), piece[1])]
+
+    def own_part(ref, side, piece):
+        start = side * (ref.shape[0] // 2) + piece[0]
+        return ref.at[pl.ds(pl.multiple_of(start, 16), piece[1])]
+
+    first = [
+        mail.post(own_part(ref, side_near, piece), part(out, narrow, side_near, piece), y_bits[0])
+        for ref, out in zip(weight_refs, weight_outs)
+        for piece in pieces(ref.shape[0])
+    ]
     rows.start()
     own_rows = rows.own()
     own_rows.start()
-    mail.post(table_ref, table_out.at[1, 0], core)
+    keeps = []
     for ref, out in zip(weight_refs, weight_outs):
-        mail.keep(ref, out.at[narrow])
+        keeps.append(mail.keep(ref, out.at[narrow]))
         mail.post(ref, out.at[narrow], core)
     own_rows.wait()
-    place = narrow
     blocks = [narrow]
     for level, bit in enumerate(y_bits):
-        fresh = []
-        arrivals = []
-        for number, (ref, out) in enumerate(zip(weight_refs, weight_outs)):
-            for spot, block in enumerate(blocks):
-                other = block + bit[1] * (1 - 2 * ((block // bit[1]) % 2))
-                if level == 0:
-                    copy = first[number]
-                else:
-                    copy = mail.post(
-                        part(out, block, side_near), part(out, block, side_near), bit
-                    )
-                arrivals.append((out, other, copy))
-                if number == 0:
-                    fresh.append(other)
+        if level:
+            for copy in keeps:
+                mail.take(copy)
+        arrivals, number = [], 0
+        for ref, out in zip(weight_refs, weight_outs):
+            for piece in pieces(ref.shape[0]):
+                for block in blocks:
+                    if level:
+                        source = part(out, block, side_near, piece)
+                        copy = mail.post(source, source, bit)
+                    else:
+                        copy = first[number]
+                        number += 1
+                    arrivals.append((out, across(block, bit), piece, copy))
         seconds = []
-        for out, other, copy in arrivals:
+        for out, other, piece, copy in arrivals:
             mail.take(copy)
-            seconds.append(
-                mail.post(part(out, other, side_near), part(out, other, side_near), near)
-            )
-            mail.post(part(out, other, side_near), part(out, other, side_near), core)
-        for (out, other, _), copy in zip(arrivals, seconds):
+            source = part(out, other, side_near, piece)
+            seconds.append(mail.post(source, source, near))
+            mail.post(source, source, core)
+        for (out, other, piece, _), copy in zip(arrivals, seconds):
             mail.take(copy)
-            mail.post(part(out, other, 1 - side_near), part(out, other, 1 - side_near), core)
-        blocks = blocks + fresh
+            source = part(out, other, 1 - side_near, piece)
+            mail.post(source, source, core)
+        blocks = blocks + [across(block, bit) for block in blocks]
 
     def hand(k):
         return pltpu.make_async_remote_copy(
@@ -829,51 +847,31 @@
         hand(k).start()
 
     rows.each(forward)
-    for level, bit in enumerate(x_bits):
-        for block in range(1 << level):
-            spot = block + (1 << level)
-            if spot not in tables:
-                tables[spot] = mail.post(table_out.at[0, block], table_out.at[0, spot], bit)
-        for block in range(1 << level):
-            spot = block + (1 << level)
-            mail.take(tables[spot])
-            mail.post(table_out.at[0, spot], table_out.at[1, spot], core)
     hand(0).wait()
     rows.each(lambda k: hand(k).wait())
     mail.close()
 
 
-def load_all(table, weights, rows):
+def load_all(weights, rows):
     lane_bits = lanes()
     sizes = chip_sizes()
     count = sizes[0] * sizes[1]
     groups = lax.axis_size("narrow")
-    across = 1 << len(lane_bits[1])
     any_space = pl.BlockSpec(memory_space=pl.ANY)
-    shapes = (
-        [jax.ShapeDtypeStruct((2, across) + table.shape, table.dtype)]
-        + [jax.ShapeDtypeStruct((groups,) + w.shape, w.dtype) for w in weights]
-        + [jax.ShapeDtypeStruct((2,) + rows.shape, rows.dtype)]
-    )
-    table_all, *weights_all, rows_all = pl.pallas_call(
+    shapes = [jax.ShapeDtypeStruct((groups,) + w.shape, w.dtype) for w in weights]
+    shapes.append(jax.ShapeDtypeStruct((2,) + rows.shape, rows.dtype))
+    *weights_all, rows_all = pl.pallas_call(
         functools.partial(load_kernel, sizes, lane_bits),
         out_shape=shapes,
-        in_specs=[pl.BlockSpec(memory_space=pltpu.VMEM)] * 6,
-        out_specs=[any_space] * 6,
-        scratch_shapes=mail_sems(8 * 2 * groups + 2 * across + 4)
-        + mail_sems(count)
-        + mail_sems(count),
+        in_specs=[pl.BlockSpec(memory_space=pltpu.VMEM)] * 5,
+        out_specs=[any_space] * 5,
+        scratch_shapes=mail_sems(8 * 4 * groups) + mail_sems(count) + mail_sems(count),
         compiler_params=pltpu.CompilerParams(
             collective_id=6, has_side_effects=True, vmem_limit_bytes=62 * MIB
         ),
         name="load_rows",
-    )(table, *weights, rows)
-    model = table.shape[1]
-    return (
-        table_all.reshape(-1, model),
-        tuple(w.reshape(-1, model) for w in weights_all),
-        rows_all,
-    )
+    )(*weights, rows)
+    return tuple(w.reshape(-1, w.shape[-1]) for w in weights_all), rows_all
 
 
 def tile_of(rows):
@@ -1170,15 +1168,61 @@
     )(array)
 
 
-def merge_stats(stats):
-    masks = group_masks()
-    rows = stats.shape[1] // 4
-    parts = exchange(stats, 1, "stats_swap", masks, False)
-    top, total, picked = (parts[:, i * rows : (i + 1) * rows] for i in range(3))
-    highest = jnp.max(top, 0)
-    own = highest + jnp.log(jnp.sum(total * jnp.exp(top - highest), 0))
-    share = exchange(jnp.pad(own, ((0, -rows % 8), (0, 0))), 8, "stats_share", masks)
-    return share[:, :rows], own, jnp.sum(picked, 0)
+def stats_kernel(masks, sizes, x_ref, target_ref, log_ref, loss_ref, got_ref, send_sem, recv_sem):
+    wides, groups = sizes
+    place = Place(wides, groups)
+    peers = [place.peer(mask // groups, mask % groups) for mask in masks]
+    greet(peers[1:])
+
+    def copy(k):
+        return pltpu.make_async_remote_copy(
+            src_ref=x_ref,
+            dst_ref=got_ref.at[k],
+            send_sem=send_sem.at[k],
+            recv_sem=recv_sem.at[k],
+            device_id=peers[k],
+            device_id_type=MESH,
+        )
+
+    blocks, height, _ = x_ref.shape
+    rows = height // 4
+    for k in range(1, blocks):
+        copy(k).start()
+    got_ref[0] = x_ref[...]
+    for k in range(1, blocks):
+        copy(k).wait()
+    for block in range(blocks):
+        parts = [got_ref[k, block ^ k] for k in range(blocks)]
+        top = functools.reduce(jnp.maximum, [part[:rows] for part in parts])
+        total = sum(part[rows : 2 * rows] * jnp.exp(part[:rows] - top) for part in parts)
+        logs = top + jnp.log(total)
+        span = pl.ds(block * rows, rows)
+        counted = target_ref[span, :] >= 0
+        log_ref[span, :] = jnp.where(counted, logs, jnp.inf)
+        if block == 0:
+            picked = sum(part[2 * rows : 3 * rows] for part in parts)
+            loss_ref[...] = jnp.where(counted, logs - picked, 0.0)
+
+
+def merge_stats(stats, targets):
+    sizes = (lax.axis_size("wide"), lax.axis_size("narrow"))
+    blocks, height, lanes_here = stats.shape
+    rows = height // 4
+    vmem = pl.BlockSpec(memory_space=pltpu.VMEM)
+    return pl.pallas_call(
+        functools.partial(stats_kernel, group_masks(), sizes),
+        out_shape=(
+            jax.ShapeDtypeStruct((blocks * rows, lanes_here), jnp.float32),
+            jax.ShapeDtypeStruct((rows, lanes_here), jnp.float32),
+        ),
+        in_specs=[vmem, vmem],
+        out_specs=(vmem, vmem),
+        scratch_shapes=[pltpu.VMEM((blocks,) + stats.shape, jnp.float32)] + mail_sems(blocks),
+        compiler_params=pltpu.CompilerParams(
+            collective_id=1, has_side_effects=True, vmem_limit_bytes=32 * MIB
+        ),
+        name="stats_share",
+    )(stats, targets)
 
 
 def put_columns(rows_ref, column_ref):
@@ -1838,10 +1882,12 @@
 
     masters = (joint_weight, output_weight, expand_weight, reduce_weight)
     served, wanted = plan(0)
-    table, weights, token_rows = load_all(
-        own_rows, [master.astype(jnp.bfloat16) for master in masters], serve(served)
-    )
-    vocab_here = table.shape[0]
+    token_rows = serve(served)
+    sent_rows, token_rows = lax.optimization_barrier((own_rows, token_rows))
+    tables = [sent_rows]
+    for bit in x_bits:
+        tables = tables + [swap(part, bit) for part in tables]
+    weights, token_rows = load_all([master.astype(jnp.bfloat16) for master in masters], token_rows)
 
     def fetch(turn):
         more, places = plan(turn)
@@ -1858,14 +1904,11 @@
     place = (differ % 2) * across + (differ // groups) % across
     rows_targets = jnp.where(is_owned, place * shard_rows + targets_group % shard_rows, -1)
     final_low, *saved = layer_forward(embedded, positions, norm_gains, bias_rows, weights)
-    group_rows = spread(final_low).reshape(-1, model_width)
+    group_rows, table = spread(final_low, tables)
     blocks = len(group_masks())
     exps, maxima, stats = head_scores(group_rows, table, rows_targets, blocks)
-    logs, own_logs, own_picked = merge_stats(stats)
-    loss_part = jnp.sum(
-        jnp.where(targets.reshape(-1, 128) >= 0, own_logs - own_picked, 0.0)
-    )
-    logs = jnp.where(targets_group >= 0, logs.reshape(-1, 128), jnp.inf)
+    logs, losses = merge_stats(stats, targets_group)
+    loss_part = jnp.sum(losses)
     slopes, final_part = head_slopes(exps, maxima, logs, rows_targets, table)
     final_grad, table_sum, passed = head_back(
         final_part.reshape(-1, tokens, model_width), slopes, group_rows

time: 595 us -> 587 us (0.987)
  Pallas kernels: 504 us -> 494 us
    pallas_call x3 -> x1, Pallas kernels: 25 us -> 11.5 us  [exchange(): pl.pallas_call(functools.partial(exchange_kernel, masks, sizes, whole), o...]
    pallas_call x1, Pallas kernels: 77.7 us -> 65.5 us  [load_all(): pl.pallas_call(functools.partial(load_kernel, sizes, lane_bits), out_shap...]
    pallas_call x0 -> x1, Pallas kernels: none -> 9.83 us  [merge_stats(): pl.pallas_call(functools.partial(stats_kernel, group_masks(), sizes), out...]
    unnamed x84 -> x88, local copies, waits for them, and re-layouts: 11.2 us -> 13.5 us
  transfers between devices with their start and end apart: 1 -> 2, of which waited for: 0 -> 0; matrix products, arithmetic and copies ran while one was open for 1% -> 3% of each run, Pallas kernels for 25% -> 39%
where the time goes in v1:
time: 587 us; the launch traced here: 578 us
  Pallas kernels  494 us (84%)
  other arithmetic  33.1 us (6%)
  local copies, waits for them, and re-layouts  22.6 us (4%)
  matrix products  16.6 us (3%)
  between operations  8.09 us (1%)
    pallas_call x1, Pallas kernels, back_reduce(): pl.pallas_call(functools.partial(back_reduce_kernel, sizes, lane_bits, ki...  149 us
    pallas_call x1, Pallas kernels, muon_factors(): pl.pallas_call(functools.partial(muon_kernel, lane_bits), out_shape=(jax....  69.5 us
    pallas_call x1, Pallas kernels, load_all(): pl.pallas_call(functools.partial(load_kernel, sizes, lane_bits), out_shap...  65.5 us
    pallas_call x1, Pallas kernels, head_back(): pl.pallas_call(functools.partial(head_back_kernel, lane_bits, plan, tile)...  48.4 us
    pallas_call x1, Pallas kernels, spread(): pl.pallas_call(functools.partial(spread_kernel, lanes(), plan), out_shape...  43.2 us
    pallas_call x1, Pallas kernels, head_scores(): pl.pallas_call(score_kernel, grid=(vocab // width,), out_shape=(jax.Shape...  35.7 us
    pallas_call x1, Pallas kernels, head_slopes(): pl.pallas_call(slope_kernel, grid=(vocab // width,), out_shape=(jax.Shape...  32.9 us
    dot_general x6, matrix products, plain(): return jnp.dot(left, right, preferred_element_type=jnp.float32)  16.4 us
  transfers between devices with their start and end apart: 2, of which 0 were waited for; matrix products, arithmetic and copies ran while one was open for 3% of the time, Pallas kernels for 39%

profile of v1, /device:TPU:0, one launch (start us, length us, event | category | flops | bytes accessed | tf_op | source)
XLA Modules:
  0.0 577.6 jit_solution(12324049799851509782)
XLA Ops:
  2.3 11.5 %label_share.1 = s32[32,8,128]{2,1,0:T(8,128)S(1)} custom-call(s32[8,128]{1,0:T(8,128)S(1)} %pad.9.x_ref), custom_call_target="tpu_custom_call" | custom-call | tf_op jit(solution)/shard_map/label_share/pallas_call | solution.py:1154
  14.2 6.3 %broadcast_compare_fusion = (pred[16,512,512]{2,1,0:T(8,128)(4,1)}, pred[16,512]{1,0:T(8,128)(4,1)S(1)}) fusion(s32[16,512]{1,0:T(8,128)S(1)} %bitcast.112, pred[512,512]{1,0:T(8,128)(4,1)S(1)} %iota_compare_fusion.18), kind=kLoop, calls=%fused_computation.28 | loop fusion | flops 12574720 | bytes 4497408 | tf_op jit(solution)/shard_map/eq | solution.py:1435
  21.5 4.1 convert_element_type.101.refs_0_
  25.6 4.4 fusion.9
  41.2 65.5 %load_rows.1 = (bf16[4,576,768]{2,1,0:T(8,128)(2,1)}, bf16[4,192,768]{2,1,0:T(8,128)(2,1)}, bf16[4,768,768]{2,1,0:T(8,128)(2,1)}, bf16[4,768,768]{2,1,0:T(8,128)(2,1)}, bf16[2,16,32,768]{3,2,1,0:T(8,128)(2,1)}) custom-call(bf16[576,768]{1,0:T(8,128)(2,1)} %convert_element_type.97.refs_0_, bf16[192,768]{1,0:T(8,128)(2,1)} %convert_element_type.98.refs_1_, ...), custom_call_target="tpu_custom_call" | custom-call | tf_op jit(solution)/shard_map/load_rows/pallas_call | solution.py:863
  106.7 2.0 fusion.21
  109.0 12.2 %layer_forward.1 = (bf16[256,768]{1,0:T(8,128)(2,1)}, f32[3,256,768]{2,1,0:T(8,128)}, f32[3,256,128]{2,1,0:T(8,128)}, bf16[256,2304]{1,0:T(8,128)(2,1)}, bf16[256,768]{1,0:T(8,128)(2,1)}, /*index=5*/f32[256,3072]{1,0:T(8,128)}) custom-call(f32[256,768]{1,0:T(8,128)S(1)} %get-tuple-element.296.x_ref, f32[64,768]{1,0:T(8,128)} %place_ref.1, f32[3,768]{1,0:T(4,128)} %refs_1_.1, ...), custom_call_target="tpu_custom_call" | custom-call | tf_op jit(solution)/shard_map/layer_forward/pallas_call | solution.py:174
  123.4 43.2 %rows_spread.1 = (bf16[8,256,768]{2,1,0:T(8,128)(2,1)}, bf16[2,2,1600,768]{3,2,1,0:T(8,128)(2,1)}) custom-call(bf16[256,768]{1,0:T(8,128)(2,1)} %get-tuple-element.301.x_ref, bf16[1600,768]{1,0:T(8,128)(2,1)} %convert_element_type.101.refs_0_, bf16[1600,768]{1,0:T(8,128)(2,1)} %collective-permute-done.2.refs_1_), custom_call_target="tpu_custom_call" | custom-call | tf_op jit(solution)/shard_map/rows_spread/pallas_call | solution.py:532
  166.6 35.7 %head_scores.1 = (bf16[2048,6400]{1,0:T(8,128)(2,1)}, f32[2048,128]{1,0:T(8,128)}, f32[8,8,128]{2,1,0:T(8,128)}) custom-call(bf16[2048,768]{1,0:T(8,128)(2,1)} %bitcast.108, bf16[6400,768]{1,0:T(8,128)(2,1)} %bitcast.121, s32[16,128]{1,0:T(8,128)} %fusion.39.target_ref), custom_call_target="tpu_custom_call" | custom-call | flops 30198988800 | bytes 26214400 | tf_op jit(solution)/shard_map/head_scores/pallas_call | solution.py:1305
  203.1 9.8 %stats_share.1 = (f32[16,128]{1,0:T(8,128)S(1)}, f32[2,128]{1,0:T(2,128)S(1)}) custom-call(f32[8,8,128]{2,1,0:T(8,128)S(1)} %copy-done, s32[16,128]{1,0:T(8,128)S(1)} %bitcast.86), custom_call_target="tpu_custom_call" | custom-call | tf_op jit(solution)/shard_map/stats_share/pallas_call | solution.py:1212
  213.5 32.9 %head_slopes.1 = (bf16[2048,6400]{1,0:T(8,128)(2,1)}, bf16[2048,768]{1,0:T(8,128)(2,1)}) custom-call(bf16[2048,6400]{1,0:T(8,128)(2,1)} %get-tuple-element.305.exps_ref, f32[2048,128]{1,0:T(8,128)} %get-tuple-element.306.max_ref, f32[16,128]{1,0:T(8,128)} %copy-done.1, s32[16,128]{1,0:T(8,128)} %fusion.39.target_ref, ...), custom_call_target="tpu_custom_call", output_to_operand_aliasing={{0}: (0, {})} | custom-call | flops 30198988800 | bytes 52428800 | tf_op jit(solution)/shard_map/head_slopes/pallas_call | solution.py:1379
  246.4 48.4 %head_back.1 = (f32[256,768]{1,0:T(8,128)}, f32[1600,768]{1,0:T(8,128)}, bf16[1600,768]{1,0:T(8,128)(2,1)}) custom-call(bf16[8,256,768]{2,1,0:T(8,128)(2,1)} %bitcast.110, bf16[2048,6400]{1,0:T(8,128)(2,1)} %get-tuple-element.310.refs_0_, bf16[2048,768]{1,0:T(8,128)(2,1)} %bitcast.109), custom_call_target="tpu_custom_call" | custom-call | tf_op jit(solution)/shard_map/head_back/pallas_call | solution.py:667
  294.8 1.5 collective-permute-start.3
  298.9 149.0 %back_reduce.1 = (bf16[768,768]{1,0:T(8,128)(2,1)}, bf16[768,768]{1,0:T(8,128)(2,1)}, bf16[768,768]{1,0:T(8,128)(2,1)}, f32[80,768]{1,0:T(8,128)}, bf16[16,32,76...) custom-call(f32[256,768]{1,0:T(8,128)} %get-tuple-element.312.refs_0_, f32[3,768]{1,0:T(4,128)} %refs_1_.1, ...), custom_call_target="tpu_custom_call" | custom-call | tf_op jit(solution)/shard_map/back_reduce/pallas_call | solution.py:1061
  447.9 16.3 %table_norm.1 = (f32[1600,768]{1,0:T(8,128)}, f32[8,128]{1,0:T(8,128)}) custom-call(f32[1600,768]{1,0:T(8,128)} %get-tuple-element.319.table_ref, bf16[1600,768]{1,0:T(8,128)(2,1)} %collective-permute-done.3.passed_ref, s32[1,512]{1,0:T(1,128)} %sub.103.slot_ref, bf16[512,768]{1,0:T(8,128)(2,1)} %bitcast.114, f32[80,768]{1,0:T(8,128)} %get-tuple-element.322.small_ref, ...), custom_call_target="tpu_custom_call" | custom-call | tf_op jit(solution)/shard_map/table_norm/pallas_call | solution.py:1550
  471.7 1.8 fusion.52
  479.2 69.5 %muon_factors.1 = (bf16[4,768,768]{2,1,0:T(8,128)(2,1)}, f32[4,8,128]{2,1,0:T(8,128)}, f32[1600,768]{1,0:T(8,128)}, f32[1600,768]{1,0:T(8,128)}, f32[1600,768]{1,0:T(8,128)}) custom-call(bf16[576,768]{1,0:T(8,128)(2,1)} %get-tuple-element.386.refs_0_, bf16[192,768]{1,0:T(8,128)(2,1)} %get-tuple-element.384.refs_1_, ...), custom_call_target="tpu_custom_call" | custom-call | tf_op jit(solution)/shard_map/muon_factors/pallas_call | solution.py:1799
  553.9 2.3 multiply_subtract_fusion.1
  556.2 3.9 add_subtract_fusion
  560.2 2.6 add_subtract_fusion.1
  564.8 2.2 multiply_subtract_fusion
  567.7 2.5 copy.68
  570.2 2.5 copy.69
  573.8 2.2 copy.70
  (144 shorter events, 37.2 us)
Async XLA Ops:
  25.6 9.3 %copy-start.6 = (f32[768,768]{1,0:T(8,128)S(1)}, f32[768,768]{1,0:T(8,128)}, u32[]{:S(2)}) copy-start(f32[768,768]{1,0:T(8,128)} %param.32) | copy-start | bytes 7077892
  30.0 93.4 %collective-permute-start.2 = (bf16[1600,768]{1,0:T(8,128)(2,1)}, bf16[1600,768]{1,0:T(8,128)(2,1)}, u32[]{:S(2)}, u32[]{:S(2)}) collective-permute-start(bf16[1600,768]{1,0:T(8,128)(2,1)} %convert_element_type.101.refs_0_), channel_id=1, source_target_pairs={{0,4},{4,0},{8,12},{12,8},{16,20},{20,16},{24,28},{28,24},{1,5},{5... | collective-permute-start | bytes 7372808 | tf_op jit(solution)/shard_map/ppermute | solution.py:347
  109.0 12.2 %copy-start.35 = (s32[4,64]{1,0:T(4,128)S(1)}, s32[4,64]{1,0:T(4,128)}, u32[]{:S(2)}) copy-start(s32[4,64]{1,0:T(4,128)} %param.28) | copy-start | bytes 3076
  294.8 153.1 %collective-permute-start.3 = (bf16[1600,768]{1,0:T(8,128)(2,1)}, bf16[1600,768]{1,0:T(8,128)(2,1)}, u32[]{:S(2)}, u32[]{:S(2)}) collective-permute-start(bf16[1600,768]{1,0:T(8,128)(2,1)} %get-tuple-element.320), channel_id=1, source_target_pairs={{0,4},{4,0},{8,12},{12,8},{16,20},{20,16},{24,28},{28,24},{1,5},{5... | collective-permute-start | bytes 7372808 | tf_op jit(solution)/shard_map/ppermute | solution.py:347
  447.9 22.7 %copy-start.24 = (bf16[768,768]{1,0:T(8,128)(2,1)S(1)}, bf16[768,768]{1,0:T(8,128)(2,1)}, u32[]{:S(2)}) copy-start(bf16[768,768]{1,0:T(8,128)(2,1)} %get-tuple-element.326) | copy-start | bytes 3538948
  447.9 22.7 %copy-start.25 = (f32[192,768]{1,0:T(8,128)S(1)}, f32[192,768]{1,0:T(8,128)}, u32[]{:S(2)}) copy-start(f32[192,768]{1,0:T(8,128)} %param.34) | copy-start | bytes 1769476
  464.2 7.5 %copy-start.21 = (f32[576,768]{1,0:T(8,128)S(1)}, f32[576,768]{1,0:T(8,128)}, u32[]{:S(2)}) copy-start(f32[576,768]{1,0:T(8,128)} %param.33) | copy-start | bytes 5308420
  476.0 80.1 %copy-start.4 = (f32[768,768]{1,0:T(8,128)}, f32[768,768]{1,0:T(8,128)S(1)}, u32[]{:S(2)}) copy-start(f32[768,768]{1,0:T(8,128)S(1)} %get-tuple-element.625) | copy-start | bytes 7077892
  478.5 81.6 %copy-start.5 = (f32[768,768]{1,0:T(8,128)}, f32[768,768]{1,0:T(8,128)S(1)}, u32[]{:S(2)}) copy-start(f32[768,768]{1,0:T(8,128)S(1)} %get-tuple-element.624) | copy-start | bytes 7077892
  479.2 73.3 %copy-start.29 = (f32[3,768]{1,0:T(4,128)S(1)}, f32[3,768]{1,0:T(4,128)}, u32[]{:S(2)}) copy-start(f32[3,768]{1,0:T(4,128)} %refs_1_.1) | copy-start | bytes 27652
  479.2 73.3 %copy-start.33 = (f32[3,768]{1,0:T(4,128)S(1)}, f32[3,768]{1,0:T(4,128)}, u32[]{:S(2)}) copy-start(f32[3,768]{1,0:T(4,128)} %param.44) | copy-start | bytes 27652
  479.2 73.3 %copy-start.34 = (f32[3,768]{1,0:T(4,128)S(1)}, f32[3,768]{1,0:T(4,128)}, u32[]{:S(2)}) copy-start(f32[3,768]{1,0:T(4,128)} %param.45) | copy-start | bytes 27652
  479.2 77.0 %copy-start.2 = (bf16[768,768]{1,0:T(8,128)(2,1)S(1)}, bf16[768,768]{1,0:T(8,128)(2,1)}, u32[]{:S(2)}) copy-start(bf16[768,768]{1,0:T(8,128)(2,1)} %get-tuple-element.380.refs_3_) | copy-start | bytes 3538948
  479.2 77.0 %copy-start.7 = (f32[768,768]{1,0:T(8,128)S(1)}, f32[768,768]{1,0:T(8,128)}, u32[]{:S(2)}) copy-start(f32[768,768]{1,0:T(8,128)} %param.32) | copy-start | bytes 7077892
  553.9 6.3 %copy-start.14 = (bf16[4,768,768]{2,1,0:T(8,128)(2,1)S(1)}, bf16[4,768,768]{2,1,0:T(8,128)(2,1)}, u32[]{:S(2)}) copy-start(bf16[4,768,768]{2,1,0:T(8,128)(2,1)} %get-tuple-element.331) | copy-start | bytes 14155780
  556.2 4.0 copy-start.3
  556.2 4.0 copy-start.9
  556.2 11.5 %slice-start.4 = ((s8[4915200]{0:T(1024)(128)(4,1)}), s8[4194304]{0:T(1024)(128)(4,1)S(1)}, s32[]{:S(2)}) async-start(s8[4915200]{0:T(1024)(128)(4,1)} %bitcast.104), calls=%async_computation.4 | async-start | bytes 8388608
  560.2 3.9 copy-start.13
  560.2 7.5 %slice-start.5 = ((s8[4915200]{0:T(1024)(128)(4,1)}), s8[720896]{0:T(1024)(128)(4,1)S(1)}, s32[]{:S(2)}) async-start(s8[4915200]{0:T(1024)(128)(4,1)} %bitcast.104), calls=%async_computation.5 | async-start | bytes 1441792
  562.8 7.4 %slice-start.2 = ((s8[4915200]{0:T(1024)(128)(4,1)}), s8[4194304]{0:T(1024)(128)(4,1)S(1)}, s32[]{:S(2)}) async-start(s8[4915200]{0:T(1024)(128)(4,1)} %bitcast.102), calls=%async_computation.2 | async-start | bytes 8388608
  564.8 5.4 slice-start.3
  567.7 5.2 slice-start
  570.2 3.6 slice-start.1
  (20 other events, 43.1 us)
